TPU v7x, 32 devices: a whole 2x2x4 slice. The times are simulated.
32 devices in a mesh: dp: 8 (over y, x, core), tensor: 4 (over z).
Axes of the slice: x: 2, y: 2, z: 4, core: 2. Of those that a mesh axis runs over, the one named last changes fastest.
Arguments:
- tokens: bfloat16 [8192, 2048], P('dp'), may hold values from -6 to 6
- segments: int32 [8192], P('dp'), may hold values from 0 to 768, as said below
- counts: int32 [8], P('dp'), may hold values from 512 to 1024, as said below
- cotangent: bfloat16 [8192, 2048], P('dp'), may hold values from -6 to 6
- attn_gain: float32 [2048], replicated, may hold values from 0.1 to 1.9
- mlp_gain: float32 [2048], replicated, may hold values from 0.1 to 1.9
- query_weight: bfloat16 [2048, 2048], P(None, 'tensor'), may hold values from -0.125 to 0.125
- key_weight: bfloat16 [2048, 256], P(None, 'tensor'), may hold values from -0.125 to 0.125
- value_weight: bfloat16 [2048, 256], P(None, 'tensor'), may hold values from -0.125 to 0.125
- out_weight: bfloat16 [2048, 2048], P('tensor'), may hold values from -0.5 to 0.5
- gate_weight: bfloat16 [2048, 5632], P(None, 'tensor'), may hold values from -0.125 to 0.125
- up_weight: bfloat16 [2048, 5632], P(None, 'tensor'), may hold values from -0.125 to 0.125
- down_weight: bfloat16 [5632, 2048], P('tensor'), may hold values from -0.125 to 0.125
Outputs:
- mixed: bfloat16 [8192, 2048], P('dp')
- tokens_grad: bfloat16 [8192, 2048], P('dp')
- attn_gain_grad: float32 [2048], P('dp')
- mlp_gain_grad: float32 [2048], P('dp')
- query_weight_grad: float32 [2048, 2048], P('dp', 'tensor')
- key_weight_grad: float32 [2048, 256], P('dp', 'tensor')
- value_weight_grad: float32 [2048, 256], P('dp', 'tensor')
- out_weight_grad: float32 [2048, 2048], P('tensor', 'dp')
- gate_weight_grad: float32 [2048, 5632], P('dp', 'tensor')
- up_weight_grad: float32 [2048, 5632], P('dp', 'tensor')
- down_weight_grad: float32 [5632, 2048], P('tensor', 'dp')
Inputs may be any that keep to these rules, and one draw needn't show every extreme that they name: `segments`: in each aligned block of 1024 tokens the ids start at 0 and never fall. `counts`: some row is fully live.
All inputs are finite; a program needn't handle non-finite values.
Results may differ from a plain program's by a relative error of at most 0.019.
Values may be sent and summed in bfloat16 or wider, within the bound.
A program may use at most 256 MiB of HBM per device.

v0:
```python
import jax
import jax.numpy as jnp
from jax import lax
from jax.sharding import PartitionSpec as P

HD = 64


EPS = 1e-05
THETA = 10000.0
NEGATIVE = -1e30


def tables(seg_row, head_dim):
    length = seg_row.shape[0]
    index = jnp.arange(length, dtype=jnp.int32)
    change = (
        jnp.concatenate(
            [jnp.ones((1,), jnp.int32), (seg_row[1:] != seg_row[:-1]).astype(jnp.int32)]
        )
        > 0
    )
    start = lax.cummax(jnp.where(change, index, 0), axis=0)
    place = (index - start).astype(jnp.float32)
    half = head_dim // 2
    freq = jnp.power(jnp.float32(THETA), -jnp.arange(half, dtype=jnp.float32) / half)
    angle = place[:, None] * freq[None, :]
    return (jnp.cos(angle), jnp.sin(angle))


def rotate(tensor, cosine, sine):
    half = tensor.shape[-1] // 2
    first = tensor[..., :half]
    second = tensor[..., half:]
    cosine = cosine[:, None, :]
    sine = sine[:, None, :]
    return jnp.concatenate(
        [first * cosine - second * sine, second * cosine + first * sine], axis=-1
    )


def unrotate(tensor, cosine, sine):
    half = tensor.shape[-1] // 2
    first = tensor[..., :half]
    second = tensor[..., half:]
    cosine = cosine[:, None, :]
    sine = sine[:, None, :]
    return jnp.concatenate(
        [first * cosine + second * sine, second * cosine - first * sine], axis=-1
    )


def normed(vector, gain):
    factor = lax.rsqrt(jnp.mean(vector * vector, axis=-1, keepdims=True) + EPS)
    return (vector * factor * gain, factor)


def norm_back(grad, vector, factor, gain):
    scaled = grad * gain
    inner = jnp.mean(scaled * vector, axis=-1, keepdims=True)
    return (
        factor * scaled - vector * (factor * factor * factor) * inner,
        jnp.sum(grad * vector * factor, axis=0),
    )


def visible_block(segments, live, begin, block):
    length = segments.shape[0]
    keys_index = jnp.arange(length, dtype=jnp.int32)
    query_index = begin + jnp.arange(block, dtype=jnp.int32)
    query_seg = segments[begin : begin + block]
    return (
        (query_seg[:, None] == segments[None, :])
        & (keys_index[None, :] <= query_index[:, None])
        & (live[None, :] | (keys_index[None, :] == query_index[:, None]))
    )


def local(
    tokens,
    segments,
    counts,
    cotangent,
    attn_gain,
    mlp_gain,
    query_weight,
    key_weight,
    value_weight,
    out_weight,
    gate_weight,
    up_weight,
    down_weight,
):
    length, width = tokens.shape
    head_dim = HD
    local_heads = query_weight.shape[1] // head_dim
    factor = head_dim ** (-0.5)
    block = min(512, length)
    xfull = tokens.astype(jnp.float32)
    hidden1_f, scale1 = normed(xfull, attn_gain)
    hidden1 = hidden1_f.astype(jnp.bfloat16)
    query_raw = jnp.dot(hidden1, query_weight, preferred_element_type=jnp.float32).reshape(
        length, local_heads, head_dim
    )
    key_raw = jnp.dot(hidden1, key_weight, preferred_element_type=jnp.float32)
    values = jnp.dot(hidden1, value_weight, preferred_element_type=jnp.float32).astype(jnp.bfloat16)
    cosine, sine = tables(segments, head_dim)
    query = rotate(query_raw, cosine, sine).astype(jnp.bfloat16)
    keys = rotate(key_raw[:, None, :], cosine, sine)[:, 0, :].astype(jnp.bfloat16)
    index = jnp.arange(length, dtype=jnp.int32)
    live = index < counts[0]
    outputs = []
    log_totals = []
    for begin in range(0, length, block):
        visible = visible_block(segments, live, begin, block)
        scores = (
            jnp.einsum(
                "qhd,kd->hqk",
                query[begin : begin + block],
                keys,
                preferred_element_type=jnp.float32,
            )
            * factor
        )
        scores = jnp.where(visible[None], scores, NEGATIVE)
        peak = jnp.max(scores, axis=-1, keepdims=True)
        weights = jnp.exp(scores - peak)
        total = jnp.sum(weights, axis=-1, keepdims=True)
        probs = (weights / total).astype(jnp.bfloat16)
        outputs.append(jnp.einsum("hqk,kd->qhd", probs, values, preferred_element_type=jnp.float32))
        log_totals.append(peak + jnp.log(total))
    heads_out = (
        jnp.concatenate(outputs, axis=0)
        .reshape(length, local_heads * head_dim)
        .astype(jnp.bfloat16)
    )
    attn_part = jnp.dot(heads_out, out_weight, preferred_element_type=jnp.float32)
    resid = xfull + lax.psum(attn_part, "tensor")
    hidden2_f, scale2 = normed(resid, mlp_gain)
    hidden2 = hidden2_f.astype(jnp.bfloat16)
    gate = jnp.dot(hidden2, gate_weight, preferred_element_type=jnp.float32)
    up_value = jnp.dot(hidden2, up_weight, preferred_element_type=jnp.float32)
    sigmoid_gate = jax.nn.sigmoid(gate)
    active = (gate * sigmoid_gate * up_value).astype(jnp.bfloat16)
    mlp_part = jnp.dot(active, down_weight, preferred_element_type=jnp.float32)
    mixed = (resid + lax.psum(mlp_part.astype(jnp.bfloat16), "tensor").astype(jnp.float32)).astype(
        jnp.bfloat16
    )
    upstream = cotangent.astype(jnp.float32) * live[:, None].astype(jnp.float32)
    upstream_low = upstream.astype(jnp.bfloat16)
    grad_down = jnp.einsum("tf,td->fd", active, upstream_low, preferred_element_type=jnp.float32)
    grad_active = jnp.einsum(
        "td,fd->tf", upstream_low, down_weight, preferred_element_type=jnp.float32
    )
    grad_gate = (
        grad_active * up_value * sigmoid_gate * (1.0 + gate * (1.0 - sigmoid_gate))
    ).astype(jnp.bfloat16)
    grad_up = (grad_active * gate * sigmoid_gate).astype(jnp.bfloat16)
    grad_gate_weight = jnp.einsum(
        "td,tf->df", hidden2, grad_gate, preferred_element_type=jnp.float32
    )
    grad_up_weight = jnp.einsum("td,tf->df", hidden2, grad_up, preferred_element_type=jnp.float32)
    grad_hidden2 = jnp.einsum(
        "tf,df->td", grad_gate, gate_weight, preferred_element_type=jnp.float32
    ) + jnp.einsum("tf,df->td", grad_up, up_weight, preferred_element_type=jnp.float32)
    grad_hidden2 = lax.psum(grad_hidden2, "tensor")
    resid_back, grad_gain2 = norm_back(grad_hidden2, resid, scale2, mlp_gain)
    grad_resid = upstream + resid_back
    grad_branch = grad_resid.astype(jnp.bfloat16)
    grad_out = jnp.einsum("tc,td->cd", heads_out, grad_branch, preferred_element_type=jnp.float32)
    grad_heads = jnp.einsum(
        "td,cd->tc", grad_branch, out_weight, preferred_element_type=jnp.float32
    )
    grad_heads = grad_heads.astype(jnp.bfloat16).reshape(length, local_heads, head_dim)
    grad_query_parts = []
    grad_keys = jnp.zeros((length, head_dim), jnp.float32)
    grad_values = jnp.zeros((length, head_dim), jnp.float32)
    for number, begin in enumerate(range(0, length, block)):
        visible = visible_block(segments, live, begin, block)
        query_block = query[begin : begin + block]
        heads_block = grad_heads[begin : begin + block]
        scores = (
            jnp.einsum("qhd,kd->hqk", query_block, keys, preferred_element_type=jnp.float32)
            * factor
        )
        scores = jnp.where(visible[None], scores, NEGATIVE)
        probs = jnp.exp(scores - log_totals[number])
        grad_probs = jnp.einsum(
            "qhd,kd->hqk", heads_block, values, preferred_element_type=jnp.float32
        )
        delta = jnp.sum(probs * grad_probs, axis=-1, keepdims=True)
        grad_scores = (probs * (grad_probs - delta)).astype(jnp.bfloat16)
        grad_query_parts.append(
            jnp.einsum("hqk,kd->qhd", grad_scores, keys, preferred_element_type=jnp.float32)
            * factor
        )
        grad_keys = (
            grad_keys
            + jnp.einsum(
                "hqk,qhd->kd", grad_scores, query_block, preferred_element_type=jnp.float32
            )
            * factor
        )
        grad_values = grad_values + jnp.einsum(
            "hqk,qhd->kd",
            probs.astype(jnp.bfloat16),
            heads_block,
            preferred_element_type=jnp.float32,
        )
    grad_query = unrotate(jnp.concatenate(grad_query_parts, axis=0), cosine, sine)
    grad_query = grad_query.reshape(length, local_heads * head_dim).astype(jnp.bfloat16)
    grad_key = unrotate(grad_keys[:, None, :], cosine, sine)[:, 0, :].astype(jnp.bfloat16)
    grad_value = grad_values.astype(jnp.bfloat16)
    grad_query_weight = jnp.einsum(
        "td,tc->dc", hidden1, grad_query, preferred_element_type=jnp.float32
    )
    grad_key_weight = jnp.einsum("td,tc->dc", hidden1, grad_key, preferred_element_type=jnp.float32)
    grad_value_weight = jnp.einsum(
        "td,tc->dc", hidden1, grad_value, preferred_element_type=jnp.float32
    )
    grad_hidden1 = (
        jnp.einsum("tc,dc->td", grad_query, query_weight, preferred_element_type=jnp.float32)
        + jnp.einsum("tc,dc->td", grad_key, key_weight, preferred_element_type=jnp.float32)
        + jnp.einsum("tc,dc->td", grad_value, value_weight, preferred_element_type=jnp.float32)
    )
    grad_hidden1 = lax.psum(grad_hidden1, "tensor")
    input_back, grad_gain1 = norm_back(grad_hidden1, xfull, scale1, attn_gain)
    tokens_grad = (grad_resid + input_back).astype(jnp.bfloat16)
    summed = (
        lax.psum_scatter(
            grad_gain1.astype(jnp.bfloat16), "dp", scatter_dimension=0, tiled=True
        ).astype(jnp.float32),
        lax.psum_scatter(
            grad_gain2.astype(jnp.bfloat16), "dp", scatter_dimension=0, tiled=True
        ).astype(jnp.float32),
        lax.psum_scatter(
            grad_query_weight.astype(jnp.bfloat16), "dp", scatter_dimension=0, tiled=True
        ).astype(jnp.float32),
        lax.psum_scatter(
            grad_key_weight.astype(jnp.bfloat16), "dp", scatter_dimension=0, tiled=True
        ).astype(jnp.float32),
        lax.psum_scatter(
            grad_value_weight.astype(jnp.bfloat16), "dp", scatter_dimension=0, tiled=True
        ).astype(jnp.float32),
        lax.psum_scatter(
            grad_out.astype(jnp.bfloat16), "dp", scatter_dimension=1, tiled=True
        ).astype(jnp.float32),
        lax.psum_scatter(
            grad_gate_weight.astype(jnp.bfloat16), "dp", scatter_dimension=0, tiled=True
        ).astype(jnp.float32),
        lax.psum_scatter(
            grad_up_weight.astype(jnp.bfloat16), "dp", scatter_dimension=0, tiled=True
        ).astype(jnp.float32),
        lax.psum_scatter(
            grad_down.astype(jnp.bfloat16), "dp", scatter_dimension=1, tiled=True
        ).astype(jnp.float32),
    )
    return (
        mixed,
        tokens_grad,
        summed[0],
        summed[1],
        summed[2],
        summed[3],
        summed[4],
        summed[5],
        summed[6],
        summed[7],
        summed[8],
    )


def solution(mesh):
    placed = (
        P("dp", None),
        P("dp"),
        P("dp"),
        P("dp", None),
        P(),
        P(),
        P(None, "tensor"),
        P(None, "tensor"),
        P(None, "tensor"),
        P("tensor", None),
        P(None, "tensor"),
        P(None, "tensor"),
        P("tensor", None),
    )
    return jax.shard_map(
        local,
        mesh=mesh,
        in_specs=placed,
        out_specs=(
            P("dp", None),
            P("dp", None),
            P("dp"),
            P("dp"),
            P("dp", "tensor"),
            P("dp", "tensor"),
            P("dp", "tensor"),
            P("tensor", "dp"),
            P("dp", "tensor"),
            P("dp", "tensor"),
            P("tensor", "dp"),
        ),
        check_vma=False,
    )
```

profile of v0, /device:TPU:0, one launch (start us, length us, event | category | flops | bytes accessed | tf_op | source)
XLA Modules:
  0.0 1568.8 jit_solution(5937977578651593383)
XLA Ops:
  10.3 3.1 fusion.14
  14.0 3.4 fusion.16
  17.4 1.4 fusion.65
  18.8 1.4 convolution_bitcast_fusion.2
  21.4 2.4 fusion.98
  24.3 2.2 fusion.33
  26.5 7.4 fusion.96
  33.9 7.3 fusion.97
  41.2 8.0 fusion.7
  49.2 7.4 fusion.49
  56.7 8.0 fusion.6
  64.7 7.6 fusion.48
  73.4 5.6 fusion.99
  79.1 293.6 %all-reduce.8.cloned.1.call-done = f32[1024,2048]{1,0:T(8,128)} async-done(((f32[1024,2048]{1,0:T(8,128)}), f32[1024,2048]{1,0:T(8,128)}) %all-reduce.8.cloned.1.call-update) | async-done | bytes 8388624 | tf_op jit(solution)/shard_map/psum | solution.py:138
  372.8 5.7 multiply_reduce_fusion.2
  379.3 12.6 fusion.101
  391.9 10.5 fusion.100
  402.4 17.2 %multiply_convert_fusion.1 = (bf16[1024,1408]{1,0:T(8,128)(2,1)}, bf16[1024,1408]{1,0:T(8,128)(2,1)}, bf16[1024,1408]{1,0:T(8,128)(2,1)}) fusion(f32[1024,1408]{1,0:T(8,128)} %fusion.100, f32[1024,1408]{1,0:T(8,128)} %fusion.101, bf16[1408,2048]{1,0:T(8,128)(2,1)} %param.25, bf16[1024,2048]{1,0:T(8,128)(2,1)} %param.16, f32[1024]{0:T(1024)S(1)} %get-tuple-element.53), kind=kOutput, calls=%fused_computation.56 | convolution fusion | flops 5934940160 | bytes 30150656 | tf_op jit(solution)/shard_map/td,fd->tf/dot_general | solution.py:152
  419.6 8.7 fusion.102
  428.3 10.7 convolution_add_fusion
  439.1 10.9 convolution_convert_fusion.3
  450.0 10.8 convolution_convert_fusion
  460.9 11.4 convolution_convert_fusion.1
  472.4 11.1 convolution_convert_fusion.2
  483.5 245.5 %all-reduce.12.cloned.1.call-done = f32[1024,2048]{1,0:T(8,128)} async-done(((f32[1024,2048]{1,0:T(8,128)}), f32[1024,2048]{1,0:T(8,128)}) %all-reduce.12.cloned.1.call-update) | async-done | bytes 8388624 | tf_op jit(solution)/shard_map/psum | solution.py:166
  729.0 7.8 multiply_reduce_fusion
  736.8 149.2 %all-reduce.10.cloned.1.call-done = bf16[1024,2048]{1,0:T(8,128)(2,1)} async-done(((bf16[1024,2048]{1,0:T(8,128)(2,1)}), bf16[1024,2048]{1,0:T(8,128)(2,1)}) %all-reduce.10.cloned.1.call-update) | async-done | bytes 4194320 | tf_op jit(solution)/shard_map/psum | solution.py:146
  886.0 15.7 %subtract_add_fusion = (f32[1024,2048]{1,0:T(8,128)}, bf16[1024,2048]{1,0:T(8,128)(2,1)}) fusion(f32[1024,2048]{1,0:T(8,128)} %copy-done.1, bf16[1024,2048]{1,0:T(8,128)(2,1)} %param.16, f32[1024,2048]{1,0:T(8,128)} %all-reduce.12.cloned.1.call-done, f32[1024]{0:T(1024)S(1)} %broadcast_multiply_fusion.1, f32[1024]{0:T(1024)S(1)} %get-tuple-element.40, ...), kind=kLoop, calls=%fused_computation.44 | loop fusion | flops 23068672 | bytes 37773312 | tf_op jit(solution)/shard_map/add | solution.py:168
  901.7 7.1 fusion.41
  908.9 2.7 fusion.53
  911.6 9.1 fusion.62
  920.7 1.6 convolution_convert_fusion.6
  922.3 13.3 fusion
  935.6 12.8 fusion.2
  948.4 3.2 copy-done.6
  951.7 2.6 convolution_bitcast_fusion
  954.4 9.5 fusion.3
  964.0 13.0 fusion.5
  977.0 3.2 copy-done.7
  980.3 2.6 fusion.52
  983.5 1.6 convolution_convert_fusion.7
  985.1 7.5 convolution_convert_fusion.4
  993.0 5.0 fusion.45
  998.0 5.5 fusion.44
  1005.0 3.8 convolution_convert_fusion.5
  1008.9 1.3 fusion.84
  1010.9 2.4 fusion.103
  1013.3 4.5 add_add_fusion
  1019.8 2.3 convert_element_type.198
  1022.1 2.4 convert_element_type.196
  1024.5 48.4 %reduce-scatter.16.cloned.1.call-done = bf16[256,1408]{1,0:T(8,128)(2,1)} async-done(((bf16[2048,1408]{1,0:T(8,128)(2,1)}), bf16[256,1408]{1,0:T(8,128)(2,1)}) %reduce-scatter.16.cloned.1.call-update) | async-done | bytes 720912 | tf_op jit(solution)/shard_map/reduce_scatter | solution.py:248
  1072.9 2.3 convert_element_type.194
  1075.2 34.4 %reduce-scatter.12.cloned.1.call-done = bf16[256,64]{0,1:T(8,128)(2,1)} async-done(((bf16[2048,64]{0,1:T(8,128)(2,1)}), bf16[256,64]{0,1:T(8,128)(2,1)}) %reduce-scatter.12.cloned.1.call-update) | async-done | bytes 32784 | tf_op jit(solution)/shard_map/reduce_scatter | solution.py:242
  1109.5 1.4 convert_element_type.190
  1110.9 36.1 %reduce-scatter.10.cloned.1.call-done = bf16[256,64]{0,1:T(8,128)(2,1)} async-done(((bf16[2048,64]{0,1:T(8,128)(2,1)}), bf16[256,64]{0,1:T(8,128)(2,1)}) %reduce-scatter.10.cloned.1.call-update) | async-done | bytes 32784 | tf_op jit(solution)/shard_map/reduce_scatter | solution.py:239
  1147.1 1.4 convert_element_type.188
  1148.5 43.1 %reduce-scatter.14.cloned.1.call-done = bf16[512,256]{1,0:T(8,128)(2,1)} async-done(((bf16[512,2048]{1,0:T(8,128)(2,1)}), bf16[512,256]{1,0:T(8,128)(2,1)}) %reduce-scatter.14.cloned.1.call-update) | async-done | bytes 262160 | tf_op jit(solution)/shard_map/reduce_scatter | solution.py:245
  1191.6 1.8 convert_element_type.192
  1193.4 43.5 %reduce-scatter.8.cloned.1.call-done = bf16[256,512]{1,0:T(8,128)(2,1)} async-done(((bf16[2048,512]{1,0:T(8,128)(2,1)}), bf16[256,512]{1,0:T(8,128)(2,1)}) %reduce-scatter.8.cloned.1.call-update) | async-done | bytes 262160 | tf_op jit(solution)/shard_map/reduce_scatter | solution.py:236
  1236.9 1.8 convert_element_type.186
  1238.7 291.5 %all-reduce.14.cloned.1.call-done = f32[1024,2048]{1,0:T(8,128)} async-done(((f32[1024,2048]{1,0:T(8,128)}), f32[1024,2048]{1,0:T(8,128)}) %all-reduce.14.cloned.1.call-update) | async-done | bytes 8388624 | tf_op jit(solution)/shard_map/psum | solution.py:226
  1530.3 6.1 fusion.23
  1536.4 13.9 all-reduce.2
  1551.6 10.3 fusion.20
  (177 shorter events, 12.6 us)
Async XLA Ops:
  7.2 66.2 %copy-start = (bf16[512,2048]{1,0:T(8,128)(2,1)S(1)}, bf16[512,2048]{1,0:T(8,128)(2,1)}, u32[]{:S(2)}) copy-start(bf16[512,2048]{1,0:T(8,128)(2,1)} %param.22) | copy-start | bytes 6291460
  7.2 10.2 copy-start.26
  7.2 365.5 %all-reduce.8.cloned.1.call-start = ((), (), s32[]{:S(2)}) async-start(), calls=%async_computation.7 | async-start | bytes 16777216 | tf_op jit(solution)/shard_map/psum | solution.py:138
  7.3 13.5 copy-start.46
  10.3 10.5 copy-start.39
  10.3 8.5 copy-start.28
  14.0 6.2 copy-start.37
  14.0 7.3 copy-start.48
  17.4 6.5 copy-start.2
  18.8 45.9 %copy-start.19 = (bf16[1024,64,1]{0,1,2:T(8,128)(2,1)}, bf16[1024,64,1]{0,1,2:T(8,128)(2,1)S(1)}, u32[]{:S(2)}) copy-start(bf16[1024,64,1]{0,1,2:T(8,128)(2,1)S(1)} %fusion.65) | copy-start | bytes 393220
  20.8 3.1 copy-start.22
  20.8 3.1 copy-start.24
  21.4 12.5 copy-start.15
  21.4 12.5 copy-start.17
  21.4 2.9 copy-start.41
  24.2 9.6 copy-start.8
  24.2 9.6 copy-start.10
  33.8 15.4 copy-start.33
  49.2 7.4 copy-start.42
  79.1 299.4 %copy-start.35 = (f32[2048]{0:T(1024)S(1)}, f32[2048]{0:T(1024)}, u32[]{:S(2)}) copy-start(f32[2048]{0:T(1024)} %param.18) | copy-start | bytes 24580
  79.1 649.9 %all-reduce.12.cloned.1.call-start = ((), (), s32[]{:S(2)}) async-start(), calls=%async_computation.9 | async-start | bytes 16777216 | tf_op jit(solution)/shard_map/psum | solution.py:166
  378.5 13.4 copy-start.1
  379.3 12.6 copy-start.14
  391.9 27.7 %slice-start.8 = ((s8[5767168]{0:T(1024)(128)(4,1)}), s8[1572864]{0:T(1024)(128)(4,1)S(1)}, s32[]{:S(2)}) async-start(s8[5767168]{0:T(1024)(128)(4,1)} %bitcast.146), calls=%async_computation.26 | async-start | bytes 3145728
  402.4 17.2 %slice-start.9 = ((s8[5767168]{0:T(1024)(128)(4,1)}), s8[4194304]{0:T(1024)(128)(4,1)S(1)}, s32[]{:S(2)}) async-start(s8[5767168]{0:T(1024)(128)(4,1)} %bitcast.146), calls=%async_computation.27 | async-start | bytes 8388608
  419.6 8.7 copy-start.51
  439.0 447.0 %all-reduce.10.cloned.1.call-start = ((), (), s32[]{:S(2)}) async-start(), calls=%async_computation.8 | async-start | bytes 8388608 | tf_op jit(solution)/shard_map/psum | solution.py:146
  449.9 569.8 %reduce-scatter.20.cloned.1.call-start = ((), (), s32[]{:S(2)}) async-start(), calls=%async_computation.17 | async-start | bytes 6488064 | tf_op jit(solution)/shard_map/reduce_scatter | solution.py:254
  460.8 11.5 copy-start.34
  460.8 11.5 copy-start.43
  460.8 561.2 %reduce-scatter.18.cloned.1.call-start = ((), (), s32[]{:S(2)}) async-start(), calls=%async_computation.16 | async-start | bytes 6488064 | tf_op jit(solution)/shard_map/reduce_scatter | solution.py:251
  472.3 600.6 %reduce-scatter.16.cloned.1.call-start = ((), (), s32[]{:S(2)}) async-start(), calls=%async_computation.15 | async-start | bytes 6488064 | tf_op jit(solution)/shard_map/reduce_scatter | solution.py:248
  483.5 626.1 %reduce-scatter.12.cloned.1.call-start = ((), (), s32[]{:S(2)}) async-start(), calls=%async_computation.13 | async-start | bytes 294912 | tf_op jit(solution)/shard_map/reduce_scatter | solution.py:242
  886.0 22.9 %slice-start = ((s8[16777216]{0:T(1024)(128)(4,1)}), s8[4194304]{0:T(1024)(128)(4,1)S(1)}, s32[]{:S(2)}) async-start(s8[16777216]{0:T(1024)(128)(4,1)} %bitcast.133), calls=%async_computation.18 | async-start | bytes 8388608
  886.0 22.9 %slice-start.1 = ((s8[16777216]{0:T(1024)(128)(4,1)}), s8[4194304]{0:T(1024)(128)(4,1)S(1)}, s32[]{:S(2)}) async-start(s8[16777216]{0:T(1024)(128)(4,1)} %bitcast.133), calls=%async_computation.19 | async-start | bytes 8388608
  886.0 22.9 %slice-start.2 = ((s8[16777216]{0:T(1024)(128)(4,1)}), s8[4194304]{0:T(1024)(128)(4,1)S(1)}, s32[]{:S(2)}) async-start(s8[16777216]{0:T(1024)(128)(4,1)} %bitcast.133), calls=%async_computation.20 | async-start | bytes 8388608
  901.7 7.2 slice-start.3
  908.8 2.8 copy-start.12
  911.6 9.2 copy-start.3
  911.6 10.7 copy-start.20
  922.3 32.0 %slice-start.4 = ((s8[16777216]{0:T(1024)(128)(4,1)}), s8[4194304]{0:T(1024)(128)(4,1)S(1)}, s32[]{:S(2)}) async-start(s8[16777216]{0:T(1024)(128)(4,1)} %bitcast.135), calls=%async_computation.22 | async-start | bytes 8388608
  922.3 32.0 %slice-start.5 = ((s8[16777216]{0:T(1024)(128)(4,1)}), s8[4194304]{0:T(1024)(128)(4,1)S(1)}, s32[]{:S(2)}) async-start(s8[16777216]{0:T(1024)(128)(4,1)} %bitcast.135), calls=%async_computation.23 | async-start | bytes 8388608
  935.6 16.1 %copy-start.9 = (bf16[1024,8,32]{0,2,1:T(8,128)(2,1)S(1)}, bf16[1024,8,32]{0,2,1:T(8,128)(2,1)}, u32[]{:S(2)}) copy-start(bf16[1024,8,32]{0,2,1:T(8,128)(2,1)} %copy-done.8) | copy-start | bytes 1572868
  935.6 16.1 %copy-start.11 = (bf16[1024,8,32]{0,2,1:T(8,128)(2,1)S(1)}, bf16[1024,8,32]{0,2,1:T(8,128)(2,1)}, u32[]{:S(2)}) copy-start(bf16[1024,8,32]{0,2,1:T(8,128)(2,1)} %copy-done.10) | copy-start | bytes 1572868
  935.6 18.8 %slice-start.6 = ((s8[16777216]{0:T(1024)(128)(4,1)}), s8[4194304]{0:T(1024)(128)(4,1)S(1)}, s32[]{:S(2)}) async-start(s8[16777216]{0:T(1024)(128)(4,1)} %bitcast.135), calls=%async_computation.24 | async-start | bytes 8388608
  935.6 18.8 %slice-start.7 = ((s8[16777216]{0:T(1024)(128)(4,1)}), s8[4194304]{0:T(1024)(128)(4,1)S(1)}, s32[]{:S(2)}) async-start(s8[16777216]{0:T(1024)(128)(4,1)} %bitcast.135), calls=%async_computation.25 | async-start | bytes 8388608
  948.4 3.2 copy-start.6
  951.7 2.7 copy-start.21
  963.9 183.1 %reduce-scatter.10.cloned.1.call-start = ((), (), s32[]{:S(2)}) async-start(), calls=%async_computation.12 | async-start | bytes 294912 | tf_op jit(solution)/shard_map/reduce_scatter | solution.py:239
  977.0 3.2 copy-start.7
  980.3 3.2 copy-start.4
  985.0 7.9 copy-start.16
  985.0 8.0 copy-start.18
  985.1 206.5 %reduce-scatter.14.cloned.1.call-start = ((), (), s32[]{:S(2)}) async-start(), calls=%async_computation.14 | async-start | bytes 2359296 | tf_op jit(solution)/shard_map/reduce_scatter | solution.py:245
  992.7 10.9 copy-start.23
  992.7 10.9 copy-start.25
  992.7 244.2 %reduce-scatter.8.cloned.1.call-start = ((), (), s32[]{:S(2)}) async-start(), calls=%async_computation.11 | async-start | bytes 2359296 | tf_op jit(solution)/shard_map/reduce_scatter | solution.py:236
  998.0 7.0 copy-start.5
  1005.0 3.9 copy-start.29
  1008.8 521.4 %all-reduce.14.cloned.1.call-start = ((), (), s32[]{:S(2)}) async-start(), calls=%async_computation.10 | async-start | bytes 16777216 | tf_op jit(solution)/shard_map/psum | solution.py:226
  1017.8 512.4 %copy-start.36 = (f32[2048]{0:T(1024)S(1)}, f32[2048]{0:T(1024)}, u32[]{:S(2)}) copy-start(f32[2048]{0:T(1024)} %param.17) | copy-start | bytes 24580
  1017.8 512.4 %copy-start.38 = (f32[1024]{0:T(1024)S(1)}, f32[1024]{0:T(1024)}, u32[]{:S(2)}) copy-start(f32[1024]{0:T(1024)} %copy-done.37) | copy-start | bytes 12292
  1024.5 511.8 %copy-start.45 = (bf16[2048]{0:T(1024)(128)(2,1)S(1)}, bf16[2048]{0:T(1024)(128)(2,1)}, u32[]{:S(2)}) copy-start(bf16[2048]{0:T(1024)(128)(2,1)} %get-tuple-element.11) | copy-start | bytes 12292
  1024.5 527.0 %copy-start.44 = (f32[1024]{0:T(1024)S(1)}, f32[1024]{0:T(1024)}, u32[]{:S(2)}) copy-start(f32[1024]{0:T(1024)} %get-tuple-element.38) | copy-start | bytes 12292
  (9 other events, 16.2 us)
Sparse Core Ops, SparseCore 0:
  79.2 293.5 all-reduce.7
  439.1 289.8 all-reduce.11
  731.9 153.9 all-reduce.9
  889.7 58.0 reduce-scatter.19
  951.0 59.1 reduce-scatter.17
  1013.9 58.9 reduce-scatter.15
  1075.9 33.5 reduce-scatter.11
  1113.4 33.5 reduce-scatter.9
  1150.4 41.2 reduce-scatter.13
  1195.7 41.2 reduce-scatter.7
  1239.4 290.8 all-reduce.13
where the time goes:
time: 1580 us; the launch traced here: 1570 us
  waiting for transfers between devices  1190 us (75%)
  matrix products  224 us (14%)
  other arithmetic  117 us (7%)
  between operations  16.5 us (1%)
    psum x1, waiting for transfers between devices, local(): resid = xfull + lax.psum(attn_part, 'tensor')  294 us
    psum x1, waiting for transfers between devices, local(): grad_hidden1 = lax.psum(grad_hidden1, 'tensor')  292 us
    psum x1, waiting for transfers between devices, local(): grad_hidden2 = lax.psum(grad_hidden2, 'tensor')  245 us
    psum x1, waiting for transfers between devices, local(): lax.psum(mlp_part.astype(jnp.bfloat16), 'tensor').astype(jnp.float32)  149 us
    reduce_scatter x1, waiting for transfers between devices, local(): lax.psum_scatter(grad_gate_weight.astype(jnp.bfloat16), 'dp', scatter_dim...  48.4 us
    reduce_scatter x1, waiting for transfers between devices, local(): lax.psum_scatter(grad_query_weight.astype(jnp.bfloat16), 'dp', scatter_di...  43.5 us
    reduce_scatter x1, waiting for transfers between devices, local(): lax.psum_scatter(grad_out.astype(jnp.bfloat16), 'dp', scatter_dimension=1...  43.1 us
    reduce_scatter x1, waiting for transfers between devices, local(): lax.psum_scatter(grad_key_weight.astype(jnp.bfloat16), 'dp', scatter_dime...  36.1 us
  transfers between devices with their start and end apart: 11, of which 9 were waited for; matrix products, arithmetic and copies ran while one was open for 12% of the time, Pallas kernels for 0%

commit v1 on v0

v1 whole, which is shorter than its diff:
```python
import functools

import jax
import jax.numpy as jnp
from jax import lax
from jax.experimental import pallas as pl
from jax.experimental.pallas import tpu as pltpu
from jax.sharding import PartitionSpec as P

HD = 64
EPS = 1e-05
THETA = 10000.0
NEGATIVE = -1e30
CHUNKS = 4
MESH = pl.DeviceIdType.MESH
BF = jnp.bfloat16
F32 = jnp.float32
ANY = pl.BlockSpec(memory_space=pl.ANY)
VMEM = pl.BlockSpec(memory_space=pltpu.VMEM)
LIMIT = 60 * 1024 * 1024


def nn(a, b):
    return lax.dot_general(a, b, (((1,), (0,)), ((), ())), preferred_element_type=F32)


def nt(a, b):
    return lax.dot_general(a, b, (((1,), (1,)), ((), ())), preferred_element_type=F32)


class Line:
    def __init__(self, piece):
        self.z = lax.axis_index("tensor")
        self.dp = lax.axis_index("dp")
        self.low = self.z < 2
        self.inner = jnp.where(self.low, self.z + 1, self.z - 1)
        self.outer = jnp.where(self.low, self.z - 1, self.z + 1)
        self.end = (self.z == 0) | (self.z == 3)
        self.mid = (self.z == 1) | (self.z == 2)
        self.piece = piece

    def at(self, m):
        place = jnp.where(self.low, m, 3 - m) * self.piece
        return pl.ds(pl.multiple_of(place, self.piece), self.piece)

    def own(self):
        return pl.ds(pl.multiple_of(self.z * self.piece, self.piece), self.piece)

    def copy(self, src, dst, send, recv, target):
        return pltpu.make_async_remote_copy(
            src_ref=src,
            dst_ref=dst,
            send_sem=send,
            recv_sem=recv,
            device_id=(self.dp, target),
            device_id_type=MESH,
        )

    def greet(self):
        barrier = pltpu.get_barrier_semaphore()
        pl.semaphore_signal(barrier, inc=1, device_id=(self.dp, self.inner), device_id_type=MESH)

        @pl.when(self.mid)
        def _():
            pl.semaphore_signal(
                barrier, inc=1, device_id=(self.dp, self.outer), device_id_type=MESH
            )
            pl.semaphore_wait(barrier, 2)

        @pl.when(self.end)
        def _():
            pl.semaphore_wait(barrier, 1)


class Reduce:
    def __init__(self, line, part, held, total, send, recv):
        self.line, self.part, self.held, self.total = line, part, held, total
        self.send, self.recv = send, recv

    def copy(self, c, m, slot, target, number):
        line = self.line
        return line.copy(
            self.part.at[c, line.at(m)],
            self.held.at[c, slot],
            self.send.at[c, number],
            self.recv.at[c, slot],
            target,
        )

    def arrived(self, c, slot):
        self.copy(c, 0, slot, self.line.inner, 0).wait_recv()

    def start(self, c):
        @pl.when(self.line.end)
        def _():
            for m in (3, 2, 1):
                self.copy(c, m, m - 1, self.line.inner, m - 1).start()

    def pass_in(self, c, m):
        line = self.line

        @pl.when(line.mid)
        def _():
            self.arrived(c, m - 1)
            rows = line.at(m)
            self.part[c, rows] = (
                self.part[c, rows].astype(F32) + self.held[c, m - 1].astype(F32)
            ).astype(BF)
            self.copy(c, m, 6 - m, line.inner, 3 - m).start()

    def pass_out(self, c):
        line = self.line

        @pl.when(line.mid)
        def _():
            self.arrived(c, 3)
            rows = line.at(0)
            self.part[c, rows] = (
                self.part[c, rows].astype(F32) + self.held[c, 3].astype(F32)
            ).astype(BF)
            self.copy(c, 0, 3, line.outer, 2).start()

    def finish(self, c):
        line = self.line

        @pl.when(line.end)
        def _():
            self.arrived(c, 3)
            self.total[...] = self.part[c, line.at(0)].astype(F32) + self.held[c, 3].astype(F32)

        @pl.when(line.mid)
        def _():
            self.arrived(c, 0)
            self.arrived(c, 4)
            self.total[...] = (
                self.part[c, line.at(1)].astype(F32)
                + self.held[c, 0].astype(F32)
                + self.held[c, 4].astype(F32)
            )

    def close(self, c):
        for number in range(3):
            self.copy(c, 0, 0, self.line.inner, number).wait_send()


class Gather:
    def __init__(self, line, own, full, send, recv, stay):
        self.line, self.own, self.full = line, own, full
        self.send, self.recv, self.stay = send, recv, stay
        self.chunk = 4 * line.piece

    def rows(self, c, m):
        line = self.line
        place = c * self.chunk + jnp.where(line.low, m, 3 - m) * line.piece
        return pl.ds(pl.multiple_of(place, line.piece), line.piece)

    def mine(self, c):
        line = self.line
        place = c * self.chunk + line.z * line.piece
        return pl.ds(pl.multiple_of(place, line.piece), line.piece)

    def first(self, c, slot, target, number):
        return self.line.copy(
            self.own.at[c],
            self.full.at[self.mine(c)],
            self.send.at[c, number],
            self.recv.at[c, slot],
            target,
        )

    def onward(self, c, m, slot, target, number):
        rows = self.rows(c, m)
        return self.line.copy(
            self.full.at[rows],
            self.full.at[rows],
            self.send.at[c, number],
            self.recv.at[c, slot],
            target,
        )

    def arrived(self, c, m):
        self.onward(c, m, m, self.line.inner, 0).wait_recv()

    def stays(self, c):
        return pltpu.make_async_copy(
            self.own.at[c], self.full.at[self.mine(c)], self.stay.at[c]
        )

    def start(self, c):
        line = self.line
        self.stays(c).start()

        @pl.when(line.end)
        def _():
            self.first(c, 0, line.inner, 0).start()

        @pl.when(line.mid)
        def _():
            self.first(c, 1, line.outer, 0).start()
            self.first(c, 2, line.inner, 1).start()

    def pass_near(self, c):
        line = self.line

        @pl.when(line.mid)
        def _():
            self.arrived(c, 0)
            self.onward(c, 0, 3, line.inner, 2).start()
            self.arrived(c, 2)
            self.onward(c, 2, 2, line.outer, 3).start()

    def pass_far(self, c):
        line = self.line

        @pl.when(line.mid)
        def _():
            self.arrived(c, 3)
            self.onward(c, 3, 3, line.outer, 4).start()

    def close(self, c):
        line = self.line
        self.stays(c).wait()

        @pl.when(line.end)
        def _():
            for m in (1, 2, 3):
                self.arrived(c, m)
            self.first(c, 0, line.inner, 0).wait_send()

        @pl.when(line.mid)
        def _():
            for number in range(5):
                self.first(c, 0, line.inner, number).wait_send()


def visible_bias(seg_row, key_row, c, chunk):
    keys = (c + 1) * chunk
    seg_q = seg_row[:, c * chunk : keys]
    seg_k = key_row[:keys, :]
    shape = (keys, chunk)
    key_at = lax.broadcasted_iota(jnp.int32, shape, 0)
    query_at = lax.broadcasted_iota(jnp.int32, shape, 1) + c * chunk
    seen = ((seg_k == seg_q) & (key_at < query_at)) | (key_at == query_at)
    return jnp.where(seen, 0.0, NEGATIVE)


def attn_kernel(
    chunks,
    tokens,
    gain,
    seg_row,
    seg_key,
    query_t,
    keys,
    values_t,
    out_weight,
    hidden2,
    resid,
    heads_out,
    logs,
    bias,
    heads_t,
    part,
    held,
    total,
    own,
    near,
    tok_sem,
    red_send,
    red_recv,
    gat_send,
    gat_recv,
    gat_stay,
):
    length, width = tokens.shape
    chunk = length // chunks
    piece = chunk // 4
    heads = query_t.shape[0] // HD
    line = Line(piece)
    red = Reduce(line, part, held, total, red_send, red_recv)
    gat = Gather(line, own, hidden2, gat_send, gat_recv, gat_stay)
    for c in range(chunks):
        pltpu.make_async_copy(tokens.at[gat.mine(c)], near.at[c], tok_sem.at[c]).start()
    line.greet()

    def attend(c):
        keys_n = (c + 1) * chunk
        cols = slice(c * chunk, keys_n)
        bias[:keys_n, :] = visible_bias(seg_row[...], seg_key[...], c, chunk)

        def head(h, carry):
            here = pl.ds(pl.multiple_of(h * HD, HD), HD)
            scores = nn(keys[:keys_n, :], query_t[here, cols]) + bias[:keys_n, :]
            peak = jnp.max(scores, axis=0, keepdims=True)
            weights = jnp.exp(scores - peak)
            sums = jnp.sum(weights, axis=0, keepdims=True)
            probs = (weights * (1.0 / sums)).astype(BF)
            heads_t[here, :] = nn(values_t[:, :keys_n], probs)
            logs[h, :, cols] = peak + jnp.log(sums)
            return carry

        lax.fori_loop(0, heads, head, 0)
        heads_c = heads_t[...].T.astype(BF)
        heads_out[cols, :] = heads_c
        step = min(512, width)
        for n in range(0, width, step):
            part[c, :, n : n + step] = nn(heads_c, out_weight[:, n : n + step]).astype(BF)

    def norm(c):
        pltpu.make_async_copy(tokens.at[gat.mine(c)], near.at[c], tok_sem.at[c]).wait()
        vector = near[c].astype(F32) + total[...]
        resid[c] = vector
        scale = lax.rsqrt(jnp.mean(vector * vector, axis=-1, keepdims=True) + EPS)
        own[c] = (vector * scale * gain[...]).astype(BF)

    order = list(reversed(range(chunks)))
    for i in range(chunks + 2):
        now = order[i] if i < chunks else None
        last = order[i - 1] if 0 <= i - 1 < chunks else None
        older = order[i - 2] if i - 2 >= 0 else None
        if now is not None:
            attend(now)
            red.start(now)
        if last is not None:
            red.pass_in(last, 3)
        if older is not None:
            gat.pass_near(older)
        if last is not None:
            red.pass_in(last, 2)
        if older is not None:
            gat.pass_far(older)
        if last is not None:
            red.pass_out(last)
            red.finish(last)
            norm(last)
            gat.start(last)
    for c in order:
        red.close(c)
        gat.close(c)


def mlp_kernel(
    chunks,
    hidden2,
    resid,
    upstream,
    gain,
    gate_weight,
    up_weight,
    down_weight,
    mixed,
    branch,
    grad_resid,
    grad_gain,
    active,
    grad_gate,
    grad_up,
    wg,
    wu,
    wd,
    hid,
    dy,
    act_c,
    gate_c,
    up_c,
    part_a,
    part_b,
    held_a,
    held_b,
    total,
    own_a,
    own_b,
    near,
    w_sem,
    in_sem,
    out_sem,
    near_sem,
    red_send_a,
    red_recv_a,
    red_send_b,
    red_recv_b,
    gat_send_a,
    gat_recv_a,
    gat_stay_a,
    gat_send_b,
    gat_recv_b,
    gat_stay_b,
):
    length, width = hidden2.shape
    chunk = length // chunks
    piece = chunk // 4
    units = wg.shape[1]
    line = Line(piece)
    red_a = Reduce(line, part_a, held_a, total, red_send_a, red_recv_a)
    red_b = Reduce(line, part_b, held_b, total, red_send_b, red_recv_b)
    gat_a = Gather(line, own_a, branch, gat_send_a, gat_recv_a, gat_stay_a)
    gat_b = Gather(line, own_b, mixed, gat_send_b, gat_recv_b, gat_stay_b)
    order = list(reversed(range(chunks)))

    def load(c, slot):
        rows = slice(c * chunk, (c + 1) * chunk)
        return (
            pltpu.make_async_copy(hidden2.at[rows], hid.at[slot], in_sem.at[slot, 0]),
            pltpu.make_async_copy(upstream.at[rows], dy.at[slot], in_sem.at[slot, 1]),
        )

    def near_copy(c):
        return pltpu.make_async_copy(upstream.at[gat_a.mine(c)], near.at[c], near_sem.at[c])

    weights = [
        pltpu.make_async_copy(src, dst, w_sem.at[i])
        for i, (src, dst) in enumerate(((gate_weight, wg), (up_weight, wu), (down_weight, wd)))
    ]
    for copy in load(order[0], 0):
        copy.start()
    for copy in weights:
        copy.start()
    for c in range(chunks):
        near_copy(c).start()
    line.greet()
    grad_gain[...] = jnp.zeros_like(grad_gain)

    def saves(c, slot):
        rows = slice(c * chunk, (c + 1) * chunk)
        return [
            pltpu.make_async_copy(src.at[slot], dst.at[rows], out_sem.at[slot, i])
            for i, (src, dst) in enumerate(((act_c, active), (gate_c, grad_gate), (up_c, grad_up)))
        ]

    def feed(i):
        c, slot = order[i], i % 2
        for copy in load(c, slot):
            copy.wait()
        if i == 0:
            for copy in weights:
                copy.wait()
        if i + 1 < chunks:
            for copy in load(order[i + 1], 1 - slot):
                copy.start()
        if i >= 2:
            for copy in saves(order[i - 2], slot):
                copy.wait()
        step = 512
        for n in range(0, units, step):
            cols = slice(n, min(n + step, units))
            gate = nn(hid[slot], wg[:, cols])
            up = nn(hid[slot], wu[:, cols])
            grad = nt(dy[slot], wd[cols, :])
            sig = 1.0 / (1.0 + jnp.exp(-gate))
            silu = gate * sig
            act_c[slot, :, cols] = (silu * up).astype(BF)
            gate_c[slot, :, cols] = (grad * up * sig * (1.0 + gate * (1.0 - sig))).astype(BF)
            up_c[slot, :, cols] = (grad * silu).astype(BF)
        for copy in saves(c, slot):
            copy.start()
        for n in range(0, width, step):
            cols = slice(n, n + step)
            part_a[c, :, cols] = (
                nt(gate_c[slot], wg[cols, :]) + nt(up_c[slot], wu[cols, :])
            ).astype(BF)
        red_a.start(c)
        for n in range(0, width, step):
            cols = slice(n, n + step)
            part_b[c, :, cols] = nn(act_c[slot], wd[:, cols]).astype(BF)

    def done_a(c):
        near_copy(c).wait()
        grad = total[...]
        vector = resid[c]
        scale = lax.rsqrt(jnp.mean(vector * vector, axis=-1, keepdims=True) + EPS)
        scaled = grad * gain[...]
        inner = jnp.mean(scaled * vector, axis=-1, keepdims=True)
        grad_gain[...] += jnp.sum(grad * vector * scale, axis=0, keepdims=True)
        back = near[c].astype(F32) + scale * scaled - vector * (scale * scale * scale) * inner
        grad_resid[c] = back
        own_a[c] = back.astype(BF)

    def done_b(c):
        own_b[c] = (resid[c] + total[...]).astype(BF)

    slots = [(red_a, gat_a, done_a, c) for c in order] + [(red_b, gat_b, done_b, c) for c in order]
    for i in range(len(slots) + 2):
        if i < chunks:
            feed(i)
        elif i < len(slots):
            red_b.start(slots[i][3])
        last = slots[i - 1] if 0 <= i - 1 < len(slots) else None
        older = slots[i - 2] if i - 2 >= 0 else None
        if last is not None:
            last[0].pass_in(last[3], 3)
        if older is not None:
            older[1].pass_near(older[3])
        if last is not None:
            last[0].pass_in(last[3], 2)
        if older is not None:
            older[1].pass_far(older[3])
        if last is not None:
            red, gat, done, c = last
            red.pass_out(c)
            red.finish(c)
            done(c)
            gat.start(c)
    for i in range(max(0, chunks - 2), chunks):
        for copy in saves(order[i], i % 2):
            copy.wait()
    for red, gat, done, c in slots:
        red.close(c)
        gat.close(c)


def back_kernel(
    chunks,
    branch,
    tokens,
    grad_resid,
    gain,
    seg_row,
    seg_key,
    cosine,
    sine,
    query_t,
    query,
    keys,
    keys_t,
    values,
    logs,
    out_weight,
    query_weight,
    kv_weight,
    tokens_grad,
    grad_gain,
    grad_query,
    grad_kv,
    bias,
    dy,
    do_t,
    do_h,
    dq_t,
    dk,
    dv,
    part,
    held,
    total,
    own,
    near,
    in_sem,
    tok_sem,
    red_send,
    red_recv,
    gat_send,
    gat_recv,
    gat_stay,
):
    length, width = tokens.shape
    chunk = length // chunks
    piece = chunk // 4
    heads = query.shape[0]
    half = HD // 2
    factor = HD ** (-0.5)
    line = Line(piece)
    red = Reduce(line, part, held, total, red_send, red_recv)
    gat = Gather(line, own, tokens_grad, gat_send, gat_recv, gat_stay)
    order = list(reversed(range(chunks)))

    def load(c, slot):
        return pltpu.make_async_copy(
            branch.at[c * chunk : (c + 1) * chunk], dy.at[slot], in_sem.at[slot]
        )

    def near_copy(c):
        return pltpu.make_async_copy(tokens.at[gat.mine(c)], near.at[c], tok_sem.at[c])

    load(order[0], 0).start()
    for c in range(chunks):
        near_copy(c).start()
    line.greet()
    grad_gain[...] = jnp.zeros_like(grad_gain)
    dk[...] = jnp.zeros_like(dk)
    dv[...] = jnp.zeros_like(dv)

    def unrope(t, cols):
        first, second = t[:half], t[half:]
        cos, sin = cosine[:, cols], sine[:, cols]
        return jnp.concatenate([first * cos + second * sin, second * cos - first * sin], axis=0)

    def attend(i):
        c, slot = order[i], i % 2
        load(c, slot).wait()
        if i + 1 < chunks:
            load(order[i + 1], 1 - slot).start()
        keys_n = (c + 1) * chunk
        cols = slice(c * chunk, keys_n)
        bias[:keys_n, :] = visible_bias(seg_row[...], seg_key[...], c, chunk)
        grad_heads = nt(dy[slot], out_weight[...])
        do_t[...] = grad_heads.T.astype(BF)
        for h in range(heads):
            do_h[h] = grad_heads[:, h * HD : (h + 1) * HD].astype(BF)

        def head(h, carry):
            here = pl.ds(pl.multiple_of(h * HD, HD), HD)
            scores = nn(keys[:keys_n, :], query_t[here, cols]) + bias[:keys_n, :]
            probs = jnp.exp(scores - logs[h, :, cols])
            grad_probs = nn(values[:keys_n, :], do_t[here, :])
            delta = jnp.sum(probs * grad_probs, axis=0, keepdims=True)
            grad_scores = (probs * (grad_probs - delta)).astype(BF)
            dv[:keys_n, :] += nn(probs.astype(BF), do_h[h])
            dk[:keys_n, :] += nn(grad_scores, query[h, cols, :])
            grad = nn(keys_t[:, :keys_n], grad_scores) * factor
            dq_t[here, :] = unrope(grad, cols)
            return carry

        lax.fori_loop(0, heads, head, 0)
        grad_q = dq_t[...].T.astype(BF)
        grad_query[cols, :] = grad_q
        grad_k = unrope(dk[cols, :].T, cols).T
        both = jnp.concatenate([grad_k, dv[cols, :]], axis=1).astype(BF)
        grad_kv[cols, :] = both
        step = min(512, width)
        for n in range(0, width, step):
            here = slice(n, n + step)
            part[c, :, here] = (
                nt(grad_q, query_weight[here, :]) + nt(both, kv_weight[here, :])
            ).astype(BF)

    def done(c):
        near_copy(c).wait()
        grad = total[...]
        vector = near[c].astype(F32)
        scale = lax.rsqrt(jnp.mean(vector * vector, axis=-1, keepdims=True) + EPS)
        scaled = grad * gain[...]
        inner = jnp.mean(scaled * vector, axis=-1, keepdims=True)
        grad_gain[...] += jnp.sum(grad * vector * scale, axis=0, keepdims=True)
        back = grad_resid[c] + scale * scaled - vector * (scale * scale * scale) * inner
        own[c] = back.astype(BF)

    for i in range(chunks + 2):
        now = order[i] if i < chunks else None
        last = order[i - 1] if 0 <= i - 1 < chunks else None
        older = order[i - 2] if i - 2 >= 0 else None
        if now is not None:
            attend(i)
            red.start(now)
        if last is not None:
            red.pass_in(last, 3)
        if older is not None:
            gat.pass_near(older)
        if last is not None:
            red.pass_in(last, 2)
        if older is not None:
            gat.pass_far(older)
        if last is not None:
            red.pass_out(last)
            red.finish(last)
            done(last)
            gat.start(last)
    for c in order:
        red.close(c)
        gat.close(c)


def call(kernel, ins, outs, scratch, number, cost):
    return pl.pallas_call(
        kernel,
        in_specs=[spec for spec, _ in ins],
        out_specs=[spec for spec, _, _ in outs],
        out_shape=[jax.ShapeDtypeStruct(shape, kind) for _, shape, kind in outs],
        scratch_shapes=scratch,
        compiler_params=pltpu.CompilerParams(
            collective_id=number, has_side_effects=True, vmem_limit_bytes=LIMIT
        ),
        cost_estimate=pl.CostEstimate(flops=cost, bytes_accessed=cost // 1000, transcendentals=0),
    )(*[array for _, array in ins])


def line_scratch(chunks, piece, width):
    dma = pltpu.SemaphoreType.DMA
    buffers = [
        pltpu.VMEM((chunks, 4 * piece, width), BF),
        pltpu.VMEM((chunks, 5, piece, width), BF),
        pltpu.VMEM((chunks, piece, width), BF),
    ]
    sems = [dma((chunks, 3)), dma((chunks, 5)), dma((chunks, 5)), dma((chunks, 4)), dma((chunks,))]
    return buffers, sems


def tables(seg_row):
    length = seg_row.shape[0]
    start = jnp.sum((seg_row[None, :] < seg_row[:, None]).astype(jnp.int32), axis=1)
    place = (jnp.arange(length, dtype=jnp.int32) - start).astype(F32)
    half = HD // 2
    freq = jnp.power(jnp.float32(THETA), -jnp.arange(half, dtype=F32) / half)
    angle = freq[:, None] * place[None, :]
    return jnp.cos(angle), jnp.sin(angle)


def rope_t(raw, cosine, sine):
    heads = raw.shape[0] // HD
    raw = raw.reshape(heads, HD, -1)
    first, second = raw[:, : HD // 2], raw[:, HD // 2 :]
    return jnp.concatenate(
        [first * cosine - second * sine, second * cosine + first * sine], axis=1
    )


def tn(a, b):
    return lax.dot_general(a, b, (((0,), (0,)), ((), ())), preferred_element_type=F32)


def local(
    tokens,
    segments,
    counts,
    cotangent,
    attn_gain,
    mlp_gain,
    query_weight,
    key_weight,
    value_weight,
    out_weight,
    gate_weight,
    up_weight,
    down_weight,
):
    length, width = tokens.shape
    units = gate_weight.shape[1]
    lanes = query_weight.shape[1]
    heads = lanes // HD
    chunks = CHUNKS
    chunk = length // chunks
    piece = chunk // 4
    dma = pltpu.SemaphoreType.DMA

    live = jnp.arange(length, dtype=jnp.int32) < counts[0]
    seg_row = segments.reshape(1, length)
    seg_key = jnp.where(live, segments, -1).reshape(length, 1)
    cosine, sine = tables(segments)
    xfull = tokens.astype(F32)
    scale1 = lax.rsqrt(jnp.mean(xfull * xfull, axis=-1, keepdims=True) + EPS)
    hidden1 = (xfull * scale1 * attn_gain).astype(BF)
    dims = (((0,), (1,)), ((), ()))
    query_raw = lax.dot_general(query_weight, hidden1, dims, preferred_element_type=F32)
    key_raw = lax.dot_general(key_weight, hidden1, dims, preferred_element_type=F32)
    values = jnp.dot(hidden1, value_weight, preferred_element_type=F32).astype(BF)
    query_h = rope_t(query_raw, cosine, sine).astype(BF) * BF(HD ** (-0.5))
    keys_t = rope_t(key_raw, cosine, sine).astype(BF)[0]
    query_t = query_h.reshape(lanes, length)
    query = query_h.transpose(0, 2, 1)
    keys = keys_t.T
    values_t = values.T
    gain1 = attn_gain.reshape(1, width)
    gain2 = mlp_gain.reshape(1, width)
    upstream = jnp.where(live[:, None], cotangent, BF(0))

    buffers, sems = line_scratch(chunks, piece, width)
    total = pltpu.VMEM((piece, width), F32)
    near = pltpu.VMEM((chunks, piece, width), BF)
    hidden2, resid, heads_out, logs = call(
        functools.partial(attn_kernel, chunks),
        [
            (ANY, tokens),
            (VMEM, gain2),
            (VMEM, seg_row),
            (VMEM, seg_key),
            (VMEM, query_t),
            (VMEM, keys),
            (VMEM, values_t),
            (VMEM, out_weight),
        ],
        [
            (ANY, (length, width), BF),
            (VMEM, (chunks, piece, width), F32),
            (VMEM, (length, lanes), BF),
            (VMEM, (heads, 1, length), F32),
        ],
        [
            pltpu.VMEM((length, chunk), F32),
            pltpu.VMEM((lanes, chunk), F32),
            buffers[0],
            buffers[1],
            total,
            buffers[2],
            near,
            dma((chunks,)),
            *sems,
        ],
        0,
        10**10,
    )

    mixed, branch, grad_resid, grad_gain2, active, grad_gate, grad_up = call(
        functools.partial(mlp_kernel, chunks),
        [
            (ANY, hidden2),
            (VMEM, resid),
            (ANY, upstream),
            (VMEM, gain2),
            (ANY, gate_weight),
            (ANY, up_weight),
            (ANY, down_weight),
        ],
        [
            (ANY, (length, width), BF),
            (ANY, (length, width), BF),
            (VMEM, (chunks, piece, width), F32),
            (VMEM, (1, width), F32),
            (ANY, (length, units), BF),
            (ANY, (length, units), BF),
            (ANY, (length, units), BF),
        ],
        [
            pltpu.VMEM((width, units), BF),
            pltpu.VMEM((width, units), BF),
            pltpu.VMEM((units, width), BF),
            pltpu.VMEM((2, chunk, width), BF),
            pltpu.VMEM((2, chunk, width), BF),
            pltpu.VMEM((2, chunk, units), BF),
            pltpu.VMEM((2, chunk, units), BF),
            pltpu.VMEM((2, chunk, units), BF),
            buffers[0],
            buffers[0],
            buffers[1],
            buffers[1],
            total,
            buffers[2],
            buffers[2],
            near,
            dma((3,)),
            dma((2, 2)),
            dma((2, 3)),
            dma((chunks,)),
            sems[0],
            sems[1],
            sems[0],
            sems[1],
            *sems[2:],
            *sems[2:],
        ],
        1,
        4 * 10**10,
    )

    tokens_grad, grad_gain1, grad_query, grad_kv = call(
        functools.partial(back_kernel, chunks),
        [
            (ANY, branch),
            (ANY, tokens),
            (VMEM, grad_resid),
            (VMEM, gain1),
            (VMEM, seg_row),
            (VMEM, seg_key),
            (VMEM, cosine),
            (VMEM, sine),
            (VMEM, query_t),
            (VMEM, query),
            (VMEM, keys),
            (VMEM, keys_t),
            (VMEM, values),
            (VMEM, logs),
            (VMEM, out_weight),
            (VMEM, query_weight),
            (VMEM, jnp.concatenate([key_weight, value_weight], axis=1)),
        ],
        [
            (ANY, (length, width), BF),
            (VMEM, (1, width), F32),
            (VMEM, (length, lanes), BF),
            (VMEM, (length, 2 * HD), BF),
        ],
        [
            pltpu.VMEM((length, chunk), F32),
            pltpu.VMEM((2, chunk, width), BF),
            pltpu.VMEM((lanes, chunk), BF),
            pltpu.VMEM((heads, chunk, HD), BF),
            pltpu.VMEM((lanes, chunk), F32),
            pltpu.VMEM((length, HD), F32),
            pltpu.VMEM((length, HD), F32),
            buffers[0],
            buffers[1],
            total,
            buffers[2],
            near,
            dma((2,)),
            dma((chunks,)),
            *sems,
        ],
        2,
        2 * 10**10,
    )

    gains = lax.psum(jnp.concatenate([grad_gain1, grad_gain2], axis=0), "tensor")
    gains = lax.psum_scatter(gains, "dp", scatter_dimension=1, tiled=True)

    def scattered(array, dim):
        return lax.psum_scatter(
            array.astype(BF), "dp", scatter_dimension=dim, tiled=True
        ).astype(F32)

    grad_qkv = tn(hidden1, jnp.concatenate([grad_query, grad_kv], axis=1))
    grad_qkv = scattered(grad_qkv, 0)
    return (
        mixed,
        tokens_grad,
        gains[0],
        gains[1],
        grad_qkv[:, :lanes],
        grad_qkv[:, lanes : lanes + HD],
        grad_qkv[:, lanes + HD :],
        scattered(tn(heads_out, branch), 1),
        scattered(tn(hidden2, grad_gate), 0),
        scattered(tn(hidden2, grad_up), 0),
        scattered(tn(active, upstream), 1),
    )


def solution(mesh):
    placed = (
        P("dp", None),
        P("dp"),
        P("dp"),
        P("dp", None),
        P(),
        P(),
        P(None, "tensor"),
        P(None, "tensor"),
        P(None, "tensor"),
        P("tensor", None),
        P(None, "tensor"),
        P(None, "tensor"),
        P("tensor", None),
    )
    return jax.shard_map(
        local,
        mesh=mesh,
        in_specs=placed,
        out_specs=(
            P("dp", None),
            P("dp", None),
            P("dp"),
            P("dp"),
            P("dp", "tensor"),
            P("dp", "tensor"),
            P("dp", "tensor"),
            P("tensor", "dp"),
            P("dp", "tensor"),
            P("dp", "tensor"),
            P("tensor", "dp"),
        ),
        check_vma=False,
    )
```

time: 1580 us -> 929 us (0.59)
  waiting for transfers between devices: 1190 us -> 244 us
  Pallas kernels: 0 us -> 536 us
  matrix products: 224 us -> 58.3 us
  other arithmetic: 117 us -> 30 us
  local copies, waits for them, and re-layouts: 10.8 us -> 30 us
    psum x4 -> x0, waiting for transfers between devices: 980 us -> none  [the longest x1 294 us: local(): resid = xfull + lax.psum(attn_part, 'tensor')]
    pallas_call x0 -> x3, Pallas kernels: none -> 536 us  [call(): pl.pallas_call(kernel, in_specs=[spec for spec, _ in ins], out_specs=[spe...]
    dot_general x33 -> x8, matrix products: 224 us -> 58.3 us  [the longest x5 46.4 us: tn(): lax.dot_general(a, b, (((0,), (0,)), ((), ())), preferred_element_type=F32)]
    convert_element_type x15 -> x5, other arithmetic: 55 us -> 8.7 us  [the longest x4 8.7 us: scattered(): return lax.psum_scatter(array.astype(BF), 'dp', scatter_dimension=dim, ti...]
    reduce_scatter x7 -> x5, waiting for transfers between devices: 206 us -> 244 us  [scattered(): lax.psum_scatter(array.astype(BF), 'dp', scatter_dimension=dim, tiled=True)]
    reduce_sum x6 -> x2, other arithmetic: 38.8 us -> 3.64 us  [the longest x1 3.08 us: local(): scale1 = lax.rsqrt(jnp.mean(xfull * xfull, axis=-1, keepdims=True) + EPS)]
  transfers between devices with their start and end apart: 11 -> 6, of which waited for: 9 -> 5; matrix products, arithmetic and copies ran while one was open for 12% -> 6% of each run, Pallas kernels for 0% -> 0%
where the time goes in v1:
time: 929 us; the launch traced here: 922 us
  Pallas kernels  536 us (58%)
  waiting for transfers between devices  244 us (26%)
  matrix products  58.3 us (6%)
  local copies, waits for them, and re-layouts  30 us (3%)
  other arithmetic  30 us (3%)
  between operations  15.5 us (2%)
    pallas_call x3, Pallas kernels, call(): pl.pallas_call(kernel, in_specs=[spec for spec, _ in ins], out_specs=[spe...  536 us
    reduce_scatter x5, waiting for transfers between devices, scattered(): lax.psum_scatter(array.astype(BF), 'dp', scatter_dimension=dim, tiled=True)  244 us
    dot_general x5, matrix products, tn(): lax.dot_general(a, b, (((0,), (0,)), ((), ())), preferred_element_type=F32)  46.4 us
    unnamed x46, local copies, waits for them, and re-layouts  20.2 us
  transfers between devices with their start and end apart: 6, of which 5 were waited for; matrix products, arithmetic and copies ran while one was open for 6% of the time, Pallas kernels for 0%

profile of v1, /device:TPU:0, one launch (start us, length us, event | category | flops | bytes accessed | tf_op | source)
XLA Modules:
  0.0 922.3 jit_solution(6809565907415187659)
XLA Ops:
  7.2 0.0 reduce-scatter.19.cloned.1.call-start
  7.3 3.1 fusion
  10.4 0.3 copy.73
  10.7 4.5 convolution_bitcast_fusion
  15.2 2.0 convolution_convert_fusion.5.values
  17.2 0.3 copy.74
  17.5 0.6 convert_reduce_fusion
  18.1 0.5 multiply_cosine_fusion.1
  18.6 1.0 copy.65
  19.6 1.0 copy.67
  20.6 5.3 fusion.22
  26.0 0.1 fusion.24
  26.2 2.9 copy.83
  29.1 2.7 copy.82
  31.8 4.6 multiply_subtract_fusion
  36.4 2.6 fusion.38.query
  39.0 1.3 fusion.3
  41.0 0.8 copy.72.values_t
  41.8 1.5 fusion.16
  43.3 0.7 pad_maximum_fusion.1
  44.0 0.8 copy.71.keys
  44.8 1.0 copy.70.seg_key
  45.9 1.6 copy.68
  47.5 1.1 pad_maximum_fusion.kv_weight
  48.6 4.6 broadcast_select_fusion.upstream
  53.1 145.8 %shard_map.212 = (bf16[1024,2048]{1,0:T(8,128)(2,1)}, f32[4,64,2048]{2,1,0:T(8,128)}, bf16[1024,512]{1,0:T(8,128)(2,1)}, f32[8,1,1024]{2,1,0:T(1,128)}) custom-call(bf16[1024,2048]{1,0:T(8,128)(2,1)} %tokens.3, f32[1,2048]{1,0:T(1,128)} %bitcast.50, s32[1,1024]{1,0:T(1,128)} %bitcast.45, s32[1024,1]{1,0:T(8,128)} %copy.70.seg_key, ...), custom_call_target="tpu_custom_call" | custom-call | flops 10000000000 | bytes 10000000 | tf_op jit(solution)/shard_map/pallas_call | solution.py:662
  198.9 245.8 %shard_map.213 = (bf16[1024,2048]{1,0:T(8,128)(2,1)}, bf16[1024,2048]{1,0:T(8,128)(2,1)}, f32[4,64,2048]{2,1,0:T(8,128)}, f32[1,2048]{1,0:T(1,128)}, bf16[1024,1...) custom-call(bf16[1024,2048]{1,0:T(8,128)(2,1)} %get-tuple-element.26.hidden2, ...), custom_call_target="tpu_custom_call" | custom-call | flops 40000000000 | bytes 40000000 | tf_op jit(solution)/shard_map/pallas_call | solution.py:662
  444.7 144.0 %shard_map.214 = (bf16[1024,2048]{1,0:T(8,128)(2,1)}, f32[1,2048]{1,0:T(1,128)}, bf16[1024,512]{1,0:T(8,128)(2,1)}, bf16[1024,128]{1,0:T(8,128)(2,1)}) custom-call(bf16[1024,2048]{1,0:T(8,128)(2,1)} %get-tuple-element.29.branch, bf16[1024,2048]{1,0:T(8,128)(2,1)} %tokens.3, f32[4,64,2048]{2,1,0:T(8,128)} %get-tuple-element.30.grad_resid, ...), custom_call_target="tpu_custom_call" | custom-call | flops 20000000000 | bytes 20000000 | tf_op jit(solution)/shard_map/pallas_call | solution.py:662
  588.7 0.7 pad_maximum_fusion.2
  589.4 1.3 copy.80
  590.8 0.0 reduce-scatter.19.cloned.1.call-update
  590.8 0.0 reduce-scatter.11.cloned.1.call-start
  590.9 5.9 convolution_convert_fusion.4
  596.8 0.0 reduce-scatter.11.cloned.1.call-update
  596.8 0.0 reduce-scatter.9.cloned.1.call-start
  596.9 8.1 convolution_convert_fusion.3
  605.0 0.0 reduce-scatter.17.cloned.1.call-start
  605.1 10.8 %convolution_convert_fusion = bf16[1408,2048]{1,0:T(8,128)(2,1)} fusion(bf16[1024,1408]{1,0:T(8,128)(2,1)S(1)} %copy-done.14, bf16[1024,2048]{1,0:T(8,128)(2,1)} %broadcast_select_fusion.upstream), kind=kOutput, calls=%fused_computation.5 | convolution fusion | flops 5908463616 | bytes 12845056 | tf_op jit(solution)/shard_map/dot_general | solution.py:706
  615.8 0.0 reduce-scatter.17.cloned.1.call-update
  615.8 0.3 reduce-scatter.13.cloned.1.call-start
  616.1 1.5 copy-done.16
  617.6 10.8 %convolution_convert_fusion.2 = bf16[2048,1408]{1,0:T(8,128)(2,1)} fusion(bf16[1024,2048]{1,0:T(8,128)(2,1)} %get-tuple-element.26.hidden2, bf16[1024,1408]{1,0:T(8,128)(2,1)S(1)} %copy-done.16), kind=kOutput, calls=%fused_computation.7 | convolution fusion | flops 5908463616 | bytes 12845056 | tf_op jit(solution)/shard_map/dot_general | solution.py:706
  628.5 0.0 reduce-scatter.15.cloned.1.call-start
  628.5 1.7 copy-done.15
  630.3 10.9 %convolution_convert_fusion.1 = bf16[2048,1408]{1,0:T(8,128)(2,1)} fusion(bf16[1024,2048]{1,0:T(8,128)(2,1)} %get-tuple-element.26.hidden2, bf16[1024,1408]{1,0:T(8,128)(2,1)S(1)} %copy-done.15), kind=kOutput, calls=%fused_computation.6 | convolution fusion | flops 5908463616 | bytes 12845056 | tf_op jit(solution)/shard_map/dot_general | solution.py:706
  641.2 0.0 reduce-scatter.19.cloned.1.call-done
  641.2 1.0 copy.81
  642.2 8.5 psum.8
  650.7 0.6 fusion.26
  651.3 18.6 %reduce-scatter.11.cloned.1.call-done = bf16[512,256]{1,0:T(8,128)(2,1)} async-done(((bf16[512,2048]{1,0:T(8,128)(2,1)}), bf16[512,256]{1,0:T(8,128)(2,1)}) %reduce-scatter.11.cloned.1.call-update) | async-done | bytes 262160 | tf_op jit(solution)/shard_map/reduce_scatter | solution.py:894
  669.9 1.8 convert_element_type.70
  671.7 46.2 %reduce-scatter.9.cloned.1.call-done = bf16[256,640]{1,0:T(8,128)(2,1)} async-done(((bf16[2048,640]{1,0:T(8,128)(2,1)}), bf16[256,640]{1,0:T(8,128)(2,1)}) %reduce-scatter.9.cloned.1.call-update) | async-done | bytes 327696 | tf_op jit(solution)/shard_map/reduce_scatter | solution.py:894
  717.8 1.0 fusion.25
  718.9 0.7 copy.78
  719.6 0.7 copy.77
  720.3 1.8 slice.42
  722.1 58.5 %reduce-scatter.17.cloned.1.call-done = bf16[1408,256]{1,0:T(8,128)(2,1)} async-done(((bf16[1408,2048]{1,0:T(8,128)(2,1)}), bf16[1408,256]{1,0:T(8,128)(2,1)}) %reduce-scatter.17.cloned.1.call-update) | async-done | bytes 720912 | tf_op jit(solution)/shard_map/reduce_scatter | solution.py:894
  780.6 2.3 convert_element_type.76
  782.9 60.1 %reduce-scatter.13.cloned.1.call-done = bf16[256,1408]{1,0:T(8,128)(2,1)} async-done(((bf16[2048,1408]{1,0:T(8,128)(2,1)}), bf16[256,1408]{1,0:T(8,128)(2,1)}) %reduce-scatter.13.cloned.1.call-update) | async-done | bytes 720912 | tf_op jit(solution)/shard_map/reduce_scatter | solution.py:894
  843.0 2.3 convert_element_type.72
  845.3 60.5 %reduce-scatter.15.cloned.1.call-done = bf16[256,1408]{1,0:T(8,128)(2,1)} async-done(((bf16[2048,1408]{1,0:T(8,128)(2,1)}), bf16[256,1408]{1,0:T(8,128)(2,1)}) %reduce-scatter.15.cloned.1.call-update) | async-done | bytes 720912 | tf_op jit(solution)/shard_map/reduce_scatter | solution.py:894
  905.7 2.3 convert_element_type.74
  908.1 4.9 copy.87
  913.0 2.0 copy.88
  (42 shorter events, 0.2 us)
Async XLA Ops:
  7.2 3.2 copy-start.6
  7.2 3.5 copy-start.11
  7.2 634.0 %reduce-scatter.19.cloned.1.call-start = ((), (), s32[]{:S(2)}) async-start(), calls=%async_computation.11 | async-start | bytes 1179648
  10.7 4.5 copy-start
  10.7 4.5 copy-start.7
  15.2 2.3 copy-start.9
  18.6 7.4 copy-start.4
  18.6 7.4 copy-start.5
  29.1 2.7 copy-start.2
  29.1 2.7 copy-start.3
  39.0 2.0 copy-start.8
  444.7 144.0 %copy-start.10 = (f32[1,2048]{1,0:T(1,128)S(1)}, f32[1,2048]{1,0:T(1,128)}, u32[]{:S(2)}) copy-start(f32[1,2048]{1,0:T(1,128)} %get-tuple-element.34) | copy-start | bytes 24580
  444.7 146.1 %copy-start.13 = (bf16[1024,512]{1,0:T(8,128)(2,1)S(1)}, bf16[1024,512]{1,0:T(8,128)(2,1)}, u32[]{:S(2)}) copy-start(bf16[1024,512]{1,0:T(8,128)(2,1)} %get-tuple-element.37) | copy-start | bytes 3145732
  590.8 79.1 %reduce-scatter.11.cloned.1.call-start = ((), (), s32[]{:S(2)}) async-start(), calls=%async_computation.7 | async-start | bytes 2359296 | tf_op jit(solution)/shard_map/reduce_scatter | solution.py:894
  590.9 6.0 copy-start.12
  590.9 6.0 copy-start.17
  596.8 121.0 %reduce-scatter.9.cloned.1.call-start = ((), (), s32[]{:S(2)}) async-start(), calls=%async_computation.6 | async-start | bytes 2949120 | tf_op jit(solution)/shard_map/reduce_scatter | solution.py:894
  596.9 8.2 copy-start.14
  605.0 175.6 %reduce-scatter.17.cloned.1.call-start = ((), (), s32[]{:S(2)}) async-start(), calls=%async_computation.10 | async-start | bytes 6488064 | tf_op jit(solution)/shard_map/reduce_scatter | solution.py:894
  615.8 1.8 copy-start.16
  615.8 227.1 %reduce-scatter.13.cloned.1.call-start = ((), (), s32[]{:S(2)}) async-start(), calls=%async_computation.8 | async-start | bytes 6488064 | tf_op jit(solution)/shard_map/reduce_scatter | solution.py:894
  628.5 1.8 copy-start.15
  628.5 277.3 %reduce-scatter.15.cloned.1.call-start = ((), (), s32[]{:S(2)}) async-start(), calls=%async_computation.9 | async-start | bytes 6488064 | tf_op jit(solution)/shard_map/reduce_scatter | solution.py:894
  908.1 4.9 copy-start.1
Sparse Core Ops, SparseCore 0:
  590.9 34.3 reduce-scatter.18
  628.6 41.2 reduce-scatter.10
  674.2 43.6 reduce-scatter.8
  721.5 59.0 reduce-scatter.16
  783.9 59.0 reduce-scatter.12
  846.7 59.0 reduce-scatter.14

commit v2 on v1

--- a/solution.py
+++ b/solution.py
@@ -28,6 +28,10 @@
     return lax.dot_general(a, b, (((1,), (1,)), ((), ())), preferred_element_type=F32)
 
 
+def tn(a, b):
+    return lax.dot_general(a, b, (((0,), (0,)), ((), ())), preferred_element_type=F32)
+
+
 class Line:
     def __init__(self, piece):
         self.z = lax.axis_index("tensor")
@@ -56,20 +60,33 @@
             device_id_type=MESH,
         )
 
-    def greet(self):
+    def greet(self, dps=2):
         barrier = pltpu.get_barrier_semaphore()
         pl.semaphore_signal(barrier, inc=1, device_id=(self.dp, self.inner), device_id_type=MESH)
+        self.groups = dps // 2
+        self.core = lax.rem(self.dp, 2)
+        self.partner = self.dp + 1 - 2 * self.core
+        others = [self.partner] + [self.peer(j) for j in range(1, self.groups)]
+        extra = 0 if dps == 2 else len(others)
+        for other in others[:extra]:
+            pl.semaphore_signal(barrier, inc=1, device_id=(other, self.z), device_id_type=MESH)
 
         @pl.when(self.mid)
         def _():
             pl.semaphore_signal(
                 barrier, inc=1, device_id=(self.dp, self.outer), device_id_type=MESH
             )
-            pl.semaphore_wait(barrier, 2)
+            pl.semaphore_wait(barrier, 2 + extra)
 
         @pl.when(self.end)
         def _():
-            pl.semaphore_wait(barrier, 1)
+            pl.semaphore_wait(barrier, 1 + extra)
+
+    def group(self, j):
+        return lax.rem(self.dp // 2 + j, self.groups)
+
+    def peer(self, j):
+        return 2 * self.group(j) + self.core
 
 
 class Reduce:
@@ -143,6 +160,101 @@
             self.copy(c, 0, 0, self.line.inner, number).wait_send()
 
 
+class Spread:
+    def __init__(self, line, stage, out, taken, sums, moved, sems):
+        self.line, self.stage, self.out = line, stage, out
+        self.taken, self.sums, self.moved = taken, sums, moved
+        self.send1, self.recv1, self.send2, self.recv2, self.stay = sems
+
+    def give(self, j):
+        line = self.line
+        return pltpu.make_async_remote_copy(
+            src_ref=self.stage.at[1 - line.core],
+            dst_ref=self.taken.at[j],
+            send_sem=self.send1.at[j],
+            recv_sem=self.recv1.at[j],
+            device_id=(line.partner, line.z),
+            device_id_type=MESH,
+        )
+
+    def move(self, j):
+        line = self.line
+        return pltpu.make_async_remote_copy(
+            src_ref=self.sums.at[j],
+            dst_ref=self.moved.at[j],
+            send_sem=self.send2.at[j],
+            recv_sem=self.recv2.at[j],
+            device_id=(line.peer(j), line.z),
+            device_id_type=MESH,
+        )
+
+    def merge_load(self, j):
+        self.give(j).wait()
+        self.load(self.taken.at[j], 1 - self.line.core).start()
+
+    def load(self, src, slot):
+        return pltpu.make_async_copy(src, self.stage.at[slot], self.stay.at[slot])
+
+    def merge_add(self, j):
+        core = self.line.core
+        self.load(self.taken.at[j], 1 - core).wait()
+        self.stage[core] = (
+            self.stage[core].astype(F32) + self.stage[1 - core].astype(F32)
+        ).astype(BF)
+        pltpu.make_async_copy(self.stage.at[core], self.sums.at[j], self.stay.at[core]).start()
+
+    def merge_move(self, j):
+        core = self.line.core
+        pltpu.make_async_copy(self.stage.at[core], self.sums.at[j], self.stay.at[core]).wait()
+        if j:
+            self.move(j).start()
+
+    def sources(self):
+        return [self.sums.at[0]] + [self.moved.at[j] for j in range(1, self.line.groups)]
+
+    def last_load(self):
+        self.load(self.sources()[0], 0).start()
+
+    def last(self):
+        sources = self.sources()
+        for j, source in enumerate(sources):
+            if j + 1 < len(sources):
+                self.move(j + 1).wait()
+                self.load(sources[j + 1], (j + 1) % 2).start()
+            self.load(source, j % 2).wait()
+            block = self.stage[j % 2].astype(F32)
+            if j:
+                self.out[...] += block
+            else:
+                self.out[...] = block
+
+
+def merged(spreads, j):
+    for spread in spreads:
+        spread.merge_load(j)
+    for spread in spreads:
+        spread.merge_add(j)
+    for spread in spreads:
+        spread.merge_move(j)
+
+
+def finished(spreads):
+    for spread in spreads:
+        spread.last_load()
+    for spread in spreads:
+        spread.last()
+
+
+def halves(stage, value, dim):
+    size = value.shape[dim] // 2
+    if dim == 0:
+        stage[0] = value[:size].astype(BF)
+        stage[1] = value[size:].astype(BF)
+    else:
+        stage[0] = value[:, :size].astype(BF)
+        stage[1] = value[:, size:].astype(BF)
+
+
 class Gather:
     def __init__(self, line, own, full, send, recv, stay):
         self.line, self.own, self.full = line, own, full
@@ -202,6 +314,10 @@
     def pass_near(self, c):
         line = self.line
 
+        @pl.when(line.end)
+        def _():
+            self.arrived(c, 1)
+
         @pl.when(line.mid)
         def _():
             self.arrived(c, 0)
@@ -223,7 +339,7 @@
 
         @pl.when(line.end)
         def _():
-            for m in (1, 2, 3):
+            for m in (2, 3):
                 self.arrived(c, m)
             self.first(c, 0, line.inner, 0).wait_send()
 
@@ -341,6 +457,7 @@
 
 def mlp_kernel(
     chunks,
+    dps,
     hidden2,
     resid,
     upstream,
@@ -352,9 +469,21 @@
     branch,
     grad_resid,
     grad_gain,
+    gate_out,
+    up_out,
+    down_out,
     active,
     grad_gate,
     grad_up,
+    gate_taken,
+    gate_sums,
+    gate_moved,
+    up_taken,
+    up_sums,
+    up_moved,
+    down_taken,
+    down_sums,
+    down_moved,
     wg,
     wu,
     wd,
@@ -365,8 +494,10 @@
     up_c,
     part_a,
     part_b,
-    held_a,
-    held_b,
+    held,
+    gate_stage,
+    up_stage,
+    down_stage,
     total,
     own_a,
     own_b,
@@ -385,14 +516,17 @@
     gat_send_b,
     gat_recv_b,
     gat_stay_b,
+    turn_sem,
+    pair_sem,
+    *dp_sems,
 ):
     length, width = hidden2.shape
     chunk = length // chunks
     piece = chunk // 4
     units = wg.shape[1]
     line = Line(piece)
-    red_a = Reduce(line, part_a, held_a, total, red_send_a, red_recv_a)
-    red_b = Reduce(line, part_b, held_b, total, red_send_b, red_recv_b)
+    red_a = Reduce(line, part_a, held, total, red_send_a, red_recv_a)
+    red_b = Reduce(line, part_b, held, total, red_send_b, red_recv_b)
     gat_a = Gather(line, own_a, branch, gat_send_a, gat_recv_a, gat_stay_a)
     gat_b = Gather(line, own_b, mixed, gat_send_b, gat_recv_b, gat_stay_b)
     order = list(reversed(range(chunks)))
@@ -417,7 +551,7 @@
         copy.start()
     for c in range(chunks):
         near_copy(c).start()
-    line.greet()
+    line.greet(dps)
     grad_gain[...] = jnp.zeros_like(grad_gain)
 
     def saves(c, slot):
@@ -463,6 +597,78 @@
             cols = slice(n, n + step)
             part_b[c, :, cols] = nn(act_c[slot], wd[:, cols]).astype(BF)
 
+    spreads = [
+        Spread(line, gate_stage, gate_out, gate_taken, gate_sums, gate_moved, dp_sems[:5]),
+        Spread(line, up_stage, up_out, up_taken, up_sums, up_moved, dp_sems[5:10]),
+        Spread(line, down_stage, down_out, down_taken, down_sums, down_moved, dp_sems[10:]),
+    ]
+    pair = 2 * width // dps
+    groups = dps // 2
+    turns = [
+        pltpu.make_async_copy(src, dst, turn_sem.at[i])
+        for i, (src, dst) in enumerate(
+            (
+                (grad_gate, wg.at[:length]),
+                (grad_up, wg.at[length : 2 * length]),
+                (active, wu.at[:length]),
+            )
+        )
+    ]
+
+    def pair_load(j, slot):
+        cols = pl.ds(pl.multiple_of(line.group(j) * pair, pair), pair)
+        at = 2 * slot * pair
+        return (
+            pltpu.make_async_copy(
+                hidden2.at[:, cols], wd.at[:length, at : at + pair], pair_sem.at[slot, 0]
+            ),
+            pltpu.make_async_copy(
+                upstream.at[:, cols],
+                wd.at[:length, at + pair : at + 2 * pair],
+                pair_sem.at[slot, 1],
+            ),
+        )
+
+    units_order = list(range(1, groups)) + [0]
+
+    def turn():
+        for i in range(max(0, chunks - 2), chunks):
+            for copy in saves(order[i], i % 2):
+                copy.wait()
+        for copy in turns:
+            copy.start()
+        for copy in pair_load(units_order[0], 0):
+            copy.start()
+
+    def unit(n):
+        j, slot = units_order[n], n % 2
+        for copy in pair_load(j, slot):
+            copy.wait()
+        if n == 0:
+            for copy in turns:
+                copy.wait()
+        if n + 1 < groups:
+            for copy in pair_load(units_order[n + 1], 1 - slot):
+                copy.start()
+        at = 2 * slot * pair
+        hid_pair = wd[:length, at : at + pair]
+        halves(gate_stage, tn(hid_pair, wg[:length, :]), 0)
+        spreads[0].give(j).start()
+        halves(up_stage, tn(hid_pair, wg[length : 2 * length, :]), 0)
+        spreads[1].give(j).start()
+        halves(down_stage, tn(wu[:length, :], wd[:length, at + pair : at + 2 * pair]), 1)
+        spreads[2].give(j).start()
+
+    work = []
+    for n in range(groups):
+        work.append(functools.partial(unit, n))
+        work.append(functools.partial(merged, spreads, units_order[n]))
+
+    def background(count=1):
+        for _ in range(count):
+            if work:
+                work.pop(0)()
+
     def done_a(c):
         near_copy(c).wait()
         grad = total[...]
@@ -484,25 +690,32 @@
             feed(i)
         elif i < len(slots):
             red_b.start(slots[i][3])
+        if i == chunks - 1:
+            turn()
+        if i >= chunks:
+            background()
         last = slots[i - 1] if 0 <= i - 1 < len(slots) else None
         older = slots[i - 2] if i - 2 >= 0 else None
         if last is not None:
             last[0].pass_in(last[3], 3)
         if older is not None:
             older[1].pass_near(older[3])
+        if i >= chunks:
+            background()
         if last is not None:
             last[0].pass_in(last[3], 2)
         if older is not None:
             older[1].pass_far(older[3])
+        if i >= chunks:
+            background()
         if last is not None:
             red, gat, done, c = last
             red.pass_out(c)
             red.finish(c)
             done(c)
             gat.start(c)
-    for i in range(max(0, chunks - 2), chunks):
-        for copy in saves(order[i], i % 2):
-            copy.wait()
+    background(len(work))
+    finished(spreads)
     for red, gat, done, c in slots:
         red.close(c)
         gat.close(c)
@@ -510,6 +723,7 @@
 
 def back_kernel(
     chunks,
+    dps,
     branch,
     tokens,
     grad_resid,
@@ -527,10 +741,23 @@
     out_weight,
     query_weight,
     kv_weight,
+    heads_out,
+    hidden1,
     tokens_grad,
     grad_gain,
-    grad_query,
-    grad_kv,
+    out_out,
+    qkv_out,
+    out_taken,
+    out_sums,
+    out_moved,
+    qkv_taken,
+    qkv_sums,
+    qkv_moved,
+    grad_qkv,
+    out_stage,
+    qkv_stage,
+    pair_out,
+    pair_qkv,
     bias,
     dy,
     do_t,
@@ -550,6 +777,8 @@
     gat_send,
     gat_recv,
     gat_stay,
+    pair_sem,
+    *dp_sems,
 ):
     length, width = tokens.shape
     chunk = length // chunks
@@ -573,7 +802,7 @@
     load(order[0], 0).start()
     for c in range(chunks):
         near_copy(c).start()
-    line.greet()
+    line.greet(dps)
     grad_gain[...] = jnp.zeros_like(grad_gain)
     dk[...] = jnp.zeros_like(dk)
     dv[...] = jnp.zeros_like(dv)
@@ -611,16 +840,58 @@
 
         lax.fori_loop(0, heads, head, 0)
         grad_q = dq_t[...].T.astype(BF)
-        grad_query[cols, :] = grad_q
+        grad_qkv[cols, : heads * HD] = grad_q
         grad_k = unrope(dk[cols, :].T, cols).T
         both = jnp.concatenate([grad_k, dv[cols, :]], axis=1).astype(BF)
-        grad_kv[cols, :] = both
+        grad_qkv[cols, heads * HD :] = both
         step = min(512, width)
         for n in range(0, width, step):
             here = slice(n, n + step)
             part[c, :, here] = (
                 nt(grad_q, query_weight[here, :]) + nt(both, kv_weight[here, :])
             ).astype(BF)
+
+    spread_out = Spread(line, out_stage, out_out, out_taken, out_sums, out_moved, dp_sems[:5])
+    spread_qkv = Spread(line, qkv_stage, qkv_out, qkv_taken, qkv_sums, qkv_moved, dp_sems[5:])
+    pair = 2 * width // dps
+    groups = dps // 2
+    units_order = list(range(1, groups)) + [0]
+
+    def pair_load(j, slot, src, dst, number):
+        cols = pl.ds(pl.multiple_of(line.group(j) * pair, pair), pair)
+        return pltpu.make_async_copy(src.at[:, cols], dst.at[slot], pair_sem.at[slot, number])
+
+    def unit_out(n):
+        j, slot = units_order[n], n % 2
+        pair_load(j, slot, branch, pair_out, 0).wait()
+        if n + 1 < groups:
+            pair_load(units_order[n + 1], 1 - slot, branch, pair_out, 0).start()
+        halves(out_stage, tn(heads_out[...], pair_out[slot]), 1)
+        spread_out.give(j).start()
+
+    def unit_qkv(n):
+        j, slot = units_order[n], n % 2
+        pair_load(j, slot, hidden1, pair_qkv, 1).wait()
+        if n + 1 < groups:
+            pair_load(units_order[n + 1], 1 - slot, hidden1, pair_qkv, 1).start()
+        halves(qkv_stage, tn(pair_qkv[slot], grad_qkv[...]), 0)
+        spread_qkv.give(j).start()
+
+    pair_load(units_order[0], 0, branch, pair_out, 0).start()
+    pair_load(units_order[0], 0, hidden1, pair_qkv, 1).start()
+    work_out, work_qkv = [], []
+    for n in range(groups):
+        work_out.append(functools.partial(unit_out, n))
+        work_out.append(functools.partial(merged, [spread_out], units_order[n]))
+        work_qkv.append(functools.partial(unit_qkv, n))
+        work_qkv.append(functools.partial(merged, [spread_qkv], units_order[n]))
+
+    def background(i, count=1):
+        for _ in range(count):
+            if work_out:
+                work_out.pop(0)()
+            elif work_qkv and i >= chunks:
+                work_qkv.pop(0)()
 
     def done(c):
         near_copy(c).wait()
@@ -642,10 +913,14 @@
             red.start(now)
         if last is not None:
             red.pass_in(last, 3)
+        if i > 0:
+            background(i)
         if older is not None:
             gat.pass_near(older)
         if last is not None:
             red.pass_in(last, 2)
+        if i > 0:
+            background(i)
         if older is not None:
             gat.pass_far(older)
         if last is not None:
@@ -653,6 +928,10 @@
             red.finish(last)
             done(last)
             gat.start(last)
+        if i > 0:
+            background(i, 2)
+    background(chunks, len(work_out) + len(work_qkv))
+    finished([spread_out, spread_qkv])
     for c in order:
         red.close(c)
         gat.close(c)
@@ -683,6 +962,14 @@
     return buffers, sems
 
 
+def spread_shapes(groups, rows, cols):
+    dma = pltpu.SemaphoreType.DMA
+    outs = [(VMEM, (rows, cols), F32)]
+    boxes = [(ANY, (groups, rows, cols), BF)] * 3
+    stage = pltpu.VMEM((2, rows, cols), BF)
+    return outs, boxes, stage, [dma((groups,))] * 4 + [dma((2,))]
+
+
 def tables(seg_row):
     length = seg_row.shape[0]
     start = jnp.sum((seg_row[None, :] < seg_row[:, None]).astype(jnp.int32), axis=1)
@@ -702,11 +989,8 @@
     )
 
 
-def tn(a, b):
-    return lax.dot_general(a, b, (((0,), (0,)), ((), ())), preferred_element_type=F32)
-
-
 def local(
+    dps,
     tokens,
     segments,
     counts,
@@ -729,6 +1013,8 @@
     chunk = length // chunks
     piece = chunk // 4
     dma = pltpu.SemaphoreType.DMA
+    groups = dps // 2
+    block = width // dps
 
     live = jnp.arange(length, dtype=jnp.int32) < counts[0]
     seg_row = segments.reshape(1, length)
@@ -787,8 +1073,10 @@
         10**10,
     )
 
-    mixed, branch, grad_resid, grad_gain2, active, grad_gate, grad_up = call(
-        functools.partial(mlp_kernel, chunks),
+    by_rows = spread_shapes(groups, block, units)
+    by_cols = spread_shapes(groups, units, block)
+    mixed, branch, grad_resid, grad_gain2, gate_grad, up_grad, down_grad, *_ = call(
+        functools.partial(mlp_kernel, chunks, dps),
         [
             (ANY, hidden2),
             (VMEM, resid),
@@ -803,9 +1091,13 @@
             (ANY, (length, width), BF),
             (VMEM, (chunks, piece, width), F32),
             (VMEM, (1, width), F32),
-            (ANY, (length, units), BF),
-            (ANY, (length, units), BF),
-            (ANY, (length, units), BF),
+            *by_rows[0],
+            *by_rows[0],
+            *by_cols[0],
+            *[(ANY, (length, units), BF)] * 3,
+            *by_rows[1],
+            *by_rows[1],
+            *by_cols[1],
         ],
         [
             pltpu.VMEM((width, units), BF),
@@ -819,7 +1111,9 @@
             buffers[0],
             buffers[0],
             buffers[1],
-            buffers[1],
+            by_rows[2],
+            by_rows[2],
+            by_cols[2],
             total,
             buffers[2],
             buffers[2],
@@ -834,13 +1128,20 @@
             sems[1],
             *sems[2:],
             *sems[2:],
+            dma((3,)),
+            dma((2, 2)),
+            *by_rows[3],
+            *by_rows[3],
+            *by_cols[3],
         ],
         1,
         4 * 10**10,
     )
 
-    tokens_grad, grad_gain1, grad_query, grad_kv = call(
-        functools.partial(back_kernel, chunks),
+    by_cols = spread_shapes(groups, lanes, block)
+    by_rows = spread_shapes(groups, block, lanes + 2 * HD)
+    tokens_grad, grad_gain1, out_grad, qkv_grad, *_ = call(
+        functools.partial(back_kernel, chunks, dps),
         [
             (ANY, branch),
             (ANY, tokens),
@@ -859,14 +1160,23 @@
             (VMEM, out_weight),
             (VMEM, query_weight),
             (VMEM, jnp.concatenate([key_weight, value_weight], axis=1)),
+            (VMEM, heads_out),
+            (ANY, hidden1),
         ],
         [
             (ANY, (length, width), BF),
             (VMEM, (1, width), F32),
-            (VMEM, (length, lanes), BF),
-            (VMEM, (length, 2 * HD), BF),
+            *by_cols[0],
+            *by_rows[0],
+            *by_cols[1],
+            *by_rows[1],
         ],
         [
+            pltpu.VMEM((length, lanes + 2 * HD), BF),
+            by_cols[2],
+            by_rows[2],
+            pltpu.VMEM((2, length, 2 * block), BF),
+            pltpu.VMEM((2, length, 2 * block), BF),
             pltpu.VMEM((length, chunk), F32),
             pltpu.VMEM((2, chunk, width), BF),
             pltpu.VMEM((lanes, chunk), BF),
@@ -882,6 +1192,9 @@
             dma((2,)),
             dma((chunks,)),
             *sems,
+            dma((2, 2)),
+            *by_cols[3],
+            *by_rows[3],
         ],
         2,
         2 * 10**10,
@@ -890,25 +1203,18 @@
     gains = lax.psum(jnp.concatenate([grad_gain1, grad_gain2], axis=0), "tensor")
     gains = lax.psum_scatter(gains, "dp", scatter_dimension=1, tiled=True)
 
-    def scattered(array, dim):
-        return lax.psum_scatter(
-            array.astype(BF), "dp", scatter_dimension=dim, tiled=True
-        ).astype(F32)
-
-    grad_qkv = tn(hidden1, jnp.concatenate([grad_query, grad_kv], axis=1))
-    grad_qkv = scattered(grad_qkv, 0)
     return (
         mixed,
         tokens_grad,
         gains[0],
         gains[1],
-        grad_qkv[:, :lanes],
-        grad_qkv[:, lanes : lanes + HD],
-        grad_qkv[:, lanes + HD :],
-        scattered(tn(heads_out, branch), 1),
-        scattered(tn(hidden2, grad_gate), 0),
-        scattered(tn(hidden2, grad_up), 0),
-        scattered(tn(active, upstream), 1),
+        qkv_grad[:, :lanes],
+        qkv_grad[:, lanes : lanes + HD],
+        qkv_grad[:, lanes + HD :],
+        out_grad,
+        gate_grad,
+        up_grad,
+        down_grad,
     )
 
 
@@ -929,7 +1235,7 @@
         P("tensor", None),
     )
     return jax.shard_map(
-        local,
+        functools.partial(local, mesh.shape["dp"]),
         mesh=mesh,
         in_specs=placed,
         out_specs=(

time: 929 us -> 694 us (0.75)
  waiting for transfers between devices: 244 us -> 34.6 us
  matrix products: 58.3 us -> 8.7 us
  Pallas kernels: 536 us -> 561 us
    reduce_scatter x5 -> x0, waiting for transfers between devices: 244 us -> none  [scattered(): lax.psum_scatter(array.astype(BF), 'dp', scatter_dimension=dim, tiled=True)]
    dot_general x5 -> x0, matrix products: 46.4 us -> none  [tn(): lax.dot_general(a, b, (((0,), (0,)), ((), ())), preferred_element_type=F32)]
    unnamed x7 -> x2, waiting for transfers between devices: 0.12 us -> 34.6 us
    pallas_call x3, Pallas kernels: 536 us -> 561 us  [call(): pl.pallas_call(kernel, in_specs=[spec for spec, _ in ins], out_specs=[spe...]
    unnamed x46 -> x48, local copies, waits for them, and re-layouts: 20.2 us -> 21.1 us
  transfers between devices with their start and end apart: 6 -> 1, of which waited for: 5 -> 1; matrix products, arithmetic and copies ran while one was open for 6% -> 1% of each run, Pallas kernels for 0% -> 0%
where the time goes in v2:
time: 694 us; the launch traced here: 687 us
  Pallas kernels  561 us (81%)
  waiting for transfers between devices  34.6 us (5%)
  local copies, waits for them, and re-layouts  32 us (5%)
  other arithmetic  23.5 us (3%)
  between operations  15.4 us (2%)
  blocking collectives  11.7 us (2%)
  matrix products  8.7 us (1%)
    pallas_call x3, Pallas kernels, call(): pl.pallas_call(kernel, in_specs=[spec for spec, _ in ins], out_specs=[spe...  561 us
    unnamed x2, waiting for transfers between devices  34.6 us
    unnamed x48, local copies, waits for them, and re-layouts  21.1 us
  transfers between devices with their start and end apart: 1, of which 1 were waited for; matrix products, arithmetic and copies ran while one was open for 1% of the time, Pallas kernels for 0%

profile of v2, /device:TPU:0, one launch (start us, length us, event | category | flops | bytes accessed | tf_op | source)
XLA Modules:
  0.0 687.1 jit_solution(15291525389579631867)
XLA Ops:
  7.2 0.0 copy-start.7
  7.2 0.0 copy-start.11
  7.2 0.0 copy-start.13
  7.2 0.0 reduce-scatter.4.cloned.1.call-start
  7.3 0.0 copy-start.15
  7.3 3.1 fusion
  10.4 0.0 copy-done.7
  10.4 0.3 copy.73
  10.7 0.0 copy-done.11
  10.7 0.3 copy.74
  11.0 0.0 copy-done.13
  11.0 3.2 fusion.2.hidden1
  14.2 0.0 copy-start
  14.2 2.1 fusion.19.values
  16.3 1.4 convolution_bitcast_fusion
  17.7 0.0 copy-done
  17.7 0.0 copy-done.12
  17.7 0.6 convert_reduce_fusion
  18.3 0.0 copy-done.15
  18.3 0.5 multiply_cosine_fusion.1
  18.8 0.0 copy-start.8
  18.9 1.0 copy.65
  19.9 1.0 copy.67
  20.9 5.2 fusion.18
  26.1 0.0 copy-done.8
  26.1 0.0 copy-done.9
  26.1 0.1 fusion.15
  26.3 2.9 copy.83
  29.2 2.7 copy.82
  31.9 0.0 copy-done.2
  31.9 4.6 multiply_subtract_fusion
  36.5 2.6 fusion.26.query
  39.1 1.3 fusion.3
  41.0 1.0 copy.70.seg_key
  42.1 1.7 copy.72.values_t
  43.8 0.6 fusion.13
  44.3 0.7 pad_maximum_fusion.1
  45.0 0.8 copy.71.keys
  45.9 1.6 copy.68
  47.5 1.1 pad_maximum_fusion.kv_weight
  48.5 4.6 broadcast_select_fusion.upstream
  53.1 145.3 %shard_map.212 = (bf16[1024,2048]{1,0:T(8,128)(2,1)}, f32[4,64,2048]{2,1,0:T(8,128)}, bf16[1024,512]{1,0:T(8,128)(2,1)}, f32[8,1,1024]{2,1,0:T(1,128)}) custom-call(bf16[1024,2048]{1,0:T(8,128)(2,1)} %tokens.3, f32[1,2048]{1,0:T(1,128)} %bitcast.48, s32[1,1024]{1,0:T(1,128)} %bitcast.42, s32[1024,1]{1,0:T(8,128)} %copy.70.seg_key, ...), custom_call_target="tpu_custom_call" | custom-call | flops 10000000000 | bytes 10000000 | tf_op jit(solution)/shard_map/pallas_call | solution.py:941
  198.4 257.9 %shard_map.213 = (bf16[1024,2048]{1,0:T(8,128)(2,1)}, bf16[1024,2048]{1,0:T(8,128)(2,1)}, f32[4,64,2048]{2,1,0:T(8,128)}, f32[1,2048]{1,0:T(1,128)}, f32[256,140...) custom-call(bf16[1024,2048]{1,0:T(8,128)(2,1)} %get-tuple-element.26, ...), custom_call_target="tpu_custom_call" | custom-call | flops 40000000000 | bytes 40000000 | tf_op jit(solution)/shard_map/pallas_call | solution.py:941
  456.3 158.1 %shard_map.214 = (bf16[1024,2048]{1,0:T(8,128)(2,1)}, f32[1,2048]{1,0:T(1,128)}, f32[512,256]{1,0:T(8,128)}, f32[256,640]{1,0:T(8,128)}, bf16[4,512,256]{2,1,0:T...) custom-call(bf16[1024,2048]{1,0:T(8,128)(2,1)} %get-tuple-element.29, ...), custom_call_target="tpu_custom_call" | custom-call | flops 20000000000 | bytes 20000000 | tf_op jit(solution)/shard_map/pallas_call | solution.py:941
  614.4 0.0 copy-done.14
  614.4 0.7 pad_maximum_fusion.2
  615.1 1.3 copy.80
  616.4 0.0 reduce-scatter.4.cloned.1.call-update
  616.5 1.1 fusion.16
  617.5 1.9 slice.33
  619.4 0.7 copy.78
  620.1 0.7 copy.77
  620.8 34.5 %reduce-scatter.4.cloned.1.call-done = f32[256,2]{1,0:T(8,128)} async-done(((f32[2048,2]{1,0:T(8,128)}), f32[256,2]{1,0:T(8,128)}) %reduce-scatter.4.cloned.1.call-update) | async-done | bytes 2064
  655.4 1.0 copy.81
  656.4 11.7 %psum.8 = f32[2,256]{1,0:T(2,128)S(1)} all-reduce(f32[2,256]{1,0:T(2,128)S(1)} %copy.81), channel_id=1, replica_groups=mesh['dp'=8,'tensor'=4] {'tensor'}, use_global_device_ids=true, to_apply=%region_2.3 | all-reduce | flops 512 | bytes 4096 | tf_op jit(solution)/shard_map/psum | solution.py:1203
  668.1 0.6 fusion.17
  668.7 4.9 copy.91
  673.6 2.1 copy.92
  675.7 0.8 copy.93
  676.5 0.0 copy-done.6
  676.5 1.1 copy.94
  677.6 1.1 copy.95
  678.7 0.0 copy-done.4
  678.7 1.1 copy.96
  (21 shorter events, 0.1 us)
Async XLA Ops:
  7.2 3.3 copy-start.7
  7.2 3.5 copy-start.11
  7.2 3.8 copy-start.13
  7.2 648.2 %reduce-scatter.4.cloned.1.call-start = ((), (), s32[]{:S(2)}) async-start(), calls=%async_computation.1 | async-start | bytes 1179648
  7.3 11.0 %copy-start.15 = (f32[32]{0:T(128)}, f32[32]{0:T(128)S(1)}, u32[]{:S(2)}) copy-start(f32[32]{0:T(128)S(1)} %multiply_power_fusion) | copy-start | bytes 388
  14.2 3.5 copy-start
  16.3 1.4 copy-start.12
  18.8 7.3 %copy-start.8 = (f32[32,1024]{1,0:T(8,128)}, f32[32,1024]{1,0:T(8,128)S(1)}, u32[]{:S(2)}) copy-start(f32[32,1024]{1,0:T(8,128)S(1)} %get-tuple-element.95.cosine) | copy-start | bytes 393220
  18.9 7.3 %copy-start.9 = (f32[32,1024]{1,0:T(8,128)}, f32[32,1024]{1,0:T(8,128)S(1)}, u32[]{:S(2)}) copy-start(f32[32,1024]{1,0:T(8,128)S(1)} %get-tuple-element.96.sine) | copy-start | bytes 393220
  29.2 2.7 copy-start.2
  29.2 2.7 copy-start.3
  39.1 4.7 copy-start.16
  456.3 158.1 %copy-start.14 = (f32[1,2048]{1,0:T(1,128)S(1)}, f32[1,2048]{1,0:T(1,128)}, u32[]{:S(2)}) copy-start(f32[1,2048]{1,0:T(1,128)} %get-tuple-element.35) | copy-start | bytes 24580
  668.6 4.9 copy-start.1
  673.6 2.1 copy-start.10
  673.6 2.9 copy-start.6
  673.6 4.0 copy-start.5
  675.7 3.0 copy-start.4
Sparse Core Ops, SparseCore 0:
  616.6 38.7 reduce-scatter.3

commit v3 on v2

v3 whole, which is shorter than its diff:
```python
import functools

import jax
import jax.numpy as jnp
from jax import lax
from jax.experimental import pallas as pl
from jax.experimental.pallas import tpu as pltpu
from jax.sharding import PartitionSpec as P

HD = 64
EPS = 1e-05
THETA = 10000.0
NEGATIVE = -1e30
CHUNKS = 8
BIG = 4
DEPTH = 4
MESH = pl.DeviceIdType.MESH
BF = jnp.bfloat16
F32 = jnp.float32
ANY = pl.BlockSpec(memory_space=pl.ANY)
VMEM = pl.BlockSpec(memory_space=pltpu.VMEM)
LIMIT = 60 * 1024 * 1024


def nn(a, b):
    return lax.dot_general(a, b, (((1,), (0,)), ((), ())), preferred_element_type=F32)


def nt(a, b):
    return lax.dot_general(a, b, (((1,), (1,)), ((), ())), preferred_element_type=F32)


def tn(a, b):
    return lax.dot_general(a, b, (((0,), (0,)), ((), ())), preferred_element_type=F32)


class Line:
    def __init__(self, piece):
        self.z = lax.axis_index("tensor")
        self.dp = lax.axis_index("dp")
        self.low = self.z < 2
        self.inner = jnp.where(self.low, self.z + 1, self.z - 1)
        self.outer = jnp.where(self.low, self.z - 1, self.z + 1)
        self.end = (self.z == 0) | (self.z == 3)
        self.mid = (self.z == 1) | (self.z == 2)
        self.piece = piece

    def at(self, m):
        place = jnp.where(self.low, m, 3 - m) * self.piece
        return pl.ds(pl.multiple_of(place, self.piece), self.piece)

    def own(self):
        return pl.ds(pl.multiple_of(self.z * self.piece, self.piece), self.piece)

    def copy(self, src, dst, send, recv, target):
        return pltpu.make_async_remote_copy(
            src_ref=src,
            dst_ref=dst,
            send_sem=send,
            recv_sem=recv,
            device_id=(self.dp, target),
            device_id_type=MESH,
        )

    def greet(self, dps, every=False):
        barrier = pltpu.get_barrier_semaphore()
        self.dps = dps
        self.groups = dps // 2
        self.core = lax.rem(self.dp, 2)
        self.partner = self.dp + 1 - 2 * self.core

        def signal(dp, z):
            pl.semaphore_signal(barrier, inc=1, device_id=(dp, z), device_id_type=MESH)

        if every:
            for j in range(1, dps):
                signal(self.dp_peer(j), self.z)
            for j in range(1, 4):
                signal(self.dp, self.z_peer(j))
            pl.semaphore_wait(barrier, dps - 1 + 3)
            return
        others = [] if dps == 2 else [self.partner] + [self.peer(j) for j in range(1, self.groups)]
        for other in others:
            signal(other, self.z)
        signal(self.dp, self.inner)

        @pl.when(self.mid)
        def _():
            signal(self.dp, self.outer)
            pl.semaphore_wait(barrier, 2 + len(others))

        @pl.when(self.end)
        def _():
            pl.semaphore_wait(barrier, 1 + len(others))

    def dp_peer(self, j):
        return lax.rem(self.dp + j, self.dps)

    def z_peer(self, j):
        return lax.rem(self.z + j, 4)

    def group(self, j):
        return lax.rem(self.dp // 2 + j, self.groups)

    def peer(self, j):
        return 2 * self.group(j) + self.core


class Reduce:
    def __init__(self, line, part, held, total, send, recv):
        self.line, self.part, self.held, self.total = line, part, held, total
        self.send, self.recv = send, recv

    def copy(self, c, m, slot, target, number):
        line = self.line
        return line.copy(
            self.part.at[c, line.at(m)],
            self.held.at[c % DEPTH, slot],
            self.send.at[c, number],
            self.recv.at[c, slot],
            target,
        )

    def arrived(self, c, slot):
        self.copy(c, 0, slot, self.line.inner, 0).wait_recv()

    def start(self, c):
        @pl.when(self.line.end)
        def _():
            for m in (3, 2, 1):
                self.copy(c, m, m - 1, self.line.inner, m - 1).start()

    def pass_in(self, c, m):
        line = self.line

        @pl.when(line.mid)
        def _():
            self.arrived(c, m - 1)
            rows = line.at(m)
            self.part[c, rows] = (
                self.part[c, rows].astype(F32) + self.held[c % DEPTH, m - 1].astype(F32)
            ).astype(BF)
            self.copy(c, m, 6 - m, line.inner, 3 - m).start()

    def pass_out(self, c):
        line = self.line

        @pl.when(line.mid)
        def _():
            self.arrived(c, 3)
            rows = line.at(0)
            self.part[c, rows] = (
                self.part[c, rows].astype(F32) + self.held[c % DEPTH, 3].astype(F32)
            ).astype(BF)
            self.copy(c, 0, 3, line.outer, 2).start()

    def finish(self, c):
        line = self.line

        @pl.when(line.end)
        def _():
            self.arrived(c, 3)
            self.total[...] = self.part[c, line.at(0)].astype(F32) + self.held[c % DEPTH, 3].astype(F32)

        @pl.when(line.mid)
        def _():
            self.arrived(c, 0)
            self.arrived(c, 4)
            self.total[...] = (
                self.part[c, line.at(1)].astype(F32)
                + self.held[c % DEPTH, 0].astype(F32)
                + self.held[c % DEPTH, 4].astype(F32)
            )

    def close(self, c):
        for number in range(3):
            self.copy(c, 0, 0, self.line.inner, number).wait_send()


class Spread:
    def __init__(self, line, stage, out, taken, sums, moved, sems):
        self.line, self.stage, self.out = line, stage, out
        self.taken, self.sums, self.moved = taken, sums, moved
        self.send1, self.recv1, self.send2, self.recv2, self.stay = sems

    def give(self, j):
        line = self.line
        return pltpu.make_async_remote_copy(
            src_ref=self.stage.at[1 - line.core],
            dst_ref=self.taken.at[j],
            send_sem=self.send1.at[j],
            recv_sem=self.recv1.at[j],
            device_id=(line.partner, line.z),
            device_id_type=MESH,
        )

    def move(self, j):
        line = self.line
        return pltpu.make_async_remote_copy(
            src_ref=self.sums.at[j],
            dst_ref=self.moved.at[j],
            send_sem=self.send2.at[j],
            recv_sem=self.recv2.at[j],
            device_id=(line.peer(j), line.z),
            device_id_type=MESH,
        )

    def merge_load(self, j):
        self.give(j).wait()
        self.load(self.taken.at[j], 1 - self.line.core).start()

    def load(self, src, slot):
        return pltpu.make_async_copy(src, self.stage.at[slot], self.stay.at[slot])

    def merge_add(self, j):
        core = self.line.core
        self.load(self.taken.at[j], 1 - core).wait()
        self.stage[core] = (
            self.stage[core].astype(F32) + self.stage[1 - core].astype(F32)
        ).astype(BF)
        pltpu.make_async_copy(self.stage.at[core], self.sums.at[j], self.stay.at[core]).start()

    def merge_move(self, j):
        core = self.line.core
        pltpu.make_async_copy(self.stage.at[core], self.sums.at[j], self.stay.at[core]).wait()
        if j:
            self.move(j).start()

    def sources(self):
        return [self.sums.at[0]] + [self.moved.at[j] for j in range(1, self.line.groups)]

    def last_load(self):
        self.load(self.sources()[0], 0).start()

    def last(self):
        sources = self.sources()
        for j, source in enumerate(sources):
            if j + 1 < len(sources):
                self.move(j + 1).wait()
                self.load(sources[j + 1], (j + 1) % 2).start()
            self.load(source, j % 2).wait()
            block = self.stage[j % 2].astype(F32)
            if j:
                self.out[...] += block
            else:
                self.out[...] = block


def merged(spreads, j):
    def run(name):
        for spread in spreads:
            getattr(spread, name)(j)

    return [functools.partial(run, name) for name in ("merge_load", "merge_add", "merge_move")]


def finished(spreads):
    for spread in spreads:
        spread.last_load()
    for spread in spreads:
        spread.last()


def halves(stage, value, dim):
    size = value.shape[dim] // 2
    if dim == 0:
        stage[0] = value[:size].astype(BF)
        stage[1] = value[size:].astype(BF)
    else:
        stage[0] = value[:, :size].astype(BF)
        stage[1] = value[:, size:].astype(BF)


class Gather:
    def __init__(self, line, own, full, send, recv, stay):
        self.line, self.own, self.full = line, own, full
        self.send, self.recv, self.stay = send, recv, stay
        self.chunk = 4 * line.piece

    def rows(self, c, m):
        line = self.line
        place = c * self.chunk + jnp.where(line.low, m, 3 - m) * line.piece
        return pl.ds(pl.multiple_of(place, line.piece), line.piece)

    def mine(self, c):
        line = self.line
        place = c * self.chunk + line.z * line.piece
        return pl.ds(pl.multiple_of(place, line.piece), line.piece)

    def first(self, c, slot, target, number):
        return self.line.copy(
            self.own.at[c],
            self.full.at[self.mine(c)],
            self.send.at[c, number],
            self.recv.at[c, slot],
            target,
        )

    def onward(self, c, m, slot, target, number):
        rows = self.rows(c, m)
        return self.line.copy(
            self.full.at[rows],
            self.full.at[rows],
            self.send.at[c, number],
            self.recv.at[c, slot],
            target,
        )

    def arrived(self, c, m):
        self.onward(c, m, m, self.line.inner, 0).wait_recv()

    def stays(self, c):
        return pltpu.make_async_copy(
            self.own.at[c], self.full.at[self.mine(c)], self.stay.at[c]
        )

    def start(self, c):
        line = self.line
        self.stays(c).start()

        @pl.when(line.end)
        def _():
            self.first(c, 0, line.inner, 0).start()

        @pl.when(line.mid)
        def _():
            self.first(c, 1, line.outer, 0).start()
            self.first(c, 2, line.inner, 1).start()

    def pass_near(self, c):
        line = self.line

        @pl.when(line.end)
        def _():
            self.arrived(c, 1)

        @pl.when(line.mid)
        def _():
            self.arrived(c, 0)
            self.onward(c, 0, 3, line.inner, 2).start()
            self.arrived(c, 2)
            self.onward(c, 2, 2, line.outer, 3).start()

    def pass_far(self, c):
        line = self.line

        @pl.when(line.mid)
        def _():
            self.arrived(c, 3)
            self.onward(c, 3, 3, line.outer, 4).start()

    def complete(self, c):
        self.stays(c).wait()

        @pl.when(self.line.end)
        def _():
            for m in (2, 3):
                self.arrived(c, m)

    def close(self, c):
        line = self.line

        @pl.when(line.end)
        def _():
            self.first(c, 0, line.inner, 0).wait_send()

        @pl.when(line.mid)
        def _():
            for number in range(5):
                self.first(c, 0, line.inner, number).wait_send()


def drive(slots, begin, plan):
    n = len(slots)
    for i in range(n + 4):
        begin(i)
        work = list(plan.get(i, ()))
        count = len(work)
        for point in range(6):
            if point == 0 and 0 <= i - 4 < n:
                _, gat, _, c = slots[i - 4]
                gat.pass_far(c)
            if point == 1 and 0 <= i - 3 < n:
                _, gat, _, c = slots[i - 3]
                gat.pass_near(c)
            if point == 2 and 0 <= i - 2 < n:
                red, gat, done, c = slots[i - 2]
                red.finish(c)
                done(c)
                gat.start(c)
            if point == 3 and 0 <= i - 1 < n:
                red, _, _, c = slots[i - 1]
                red.pass_out(c)
            if point == 4 and i < n:
                red, _, _, c = slots[i]
                red.pass_in(c, 3)
            if point == 5 and i < n:
                red, _, _, c = slots[i]
                red.pass_in(c, 2)
            while work and count - len(work) < (point + 1) * count // 6:
                work.pop(0)()
        for task in work:
            task()


def schedule(plan, tasks, first, per_step):
    for k, task in enumerate(tasks):
        plan.setdefault(first + k // per_step, []).append(task)


def put(part, big, cols, value):
    chunk = part.shape[1]
    sub = value.shape[0] // chunk
    for k in range(sub):
        part[big * sub + k, :, cols] = value[k * chunk : (k + 1) * chunk].astype(BF)


def rope(t, cos, sin):
    half = HD // 2
    first, second = t[:half], t[half:]
    return jnp.concatenate([first * cos - second * sin, second * cos + first * sin], axis=0)


def unrope(t, cos, sin):
    half = HD // 2
    first, second = t[:half], t[half:]
    return jnp.concatenate([first * cos + second * sin, second * cos - first * sin], axis=0)


def normed(vector):
    return lax.rsqrt(jnp.mean(vector * vector, axis=-1, keepdims=True) + EPS)


def visible_bias(seg_row, key_row, c, chunk):
    keys = (c + 1) * chunk
    seg_q = seg_row[:, c * chunk : keys]
    seg_k = key_row[:keys, :]
    shape = (keys, chunk)
    key_at = lax.broadcasted_iota(jnp.int32, shape, 0)
    query_at = lax.broadcasted_iota(jnp.int32, shape, 1) + c * chunk
    seen = ((seg_k == seg_q) & (key_at < query_at)) | (key_at == query_at)
    return jnp.where(seen, 0.0, NEGATIVE)


def front_kernel(
    chunks,
    big,
    dps,
    tokens,
    cotangent,
    live,
    gain1,
    gain2,
    seg_row,
    seg_key,
    cosine,
    sine,
    query_weight,
    kv_weight,
    out_weight,
    gate_weight,
    up_weight,
    down_weight,
    mixed,
    branch,
    hidden1,
    grad_resid,
    grad_gain,
    heads_out,
    logs,
    query_t,
    keys,
    keys_t,
    values,
    gate_out,
    up_out,
    down_out,
    hidden2,
    active,
    grad_gate,
    grad_up,
    gate_taken,
    gate_sums,
    gate_moved,
    up_taken,
    up_sums,
    up_moved,
    down_taken,
    down_sums,
    down_moved,
    wg,
    wu,
    wd,
    hid,
    dy,
    act_c,
    gate_c,
    up_c,
    gate_stage,
    up_stage,
    down_stage,
    values_t,
    bias,
    heads_t,
    resid,
    part_p,
    part_a,
    held,
    own_p,
    own_a,
    near,
    total,
    w_sem,
    in_sem,
    out_sem,
    save_sem,
    near_sem,
    turn_sem,
    pair_sem,
    *sems,
):
    length, width = tokens.shape
    units = wg.shape[1]
    chunk = length // chunks
    wide = length // big
    sub = chunks // big
    piece = chunk // 4
    lanes = query_t.shape[0]
    heads = lanes // HD
    if gate_stage.shape[1] != width // dps:
        gate_stage, up_stage = gate_c, up_c
    line = Line(piece)
    red_p = Reduce(line, part_p, held, total, *sems[0:2])
    gat_p = Gather(line, own_p, hidden2, *sems[2:5])
    red_a = Reduce(line, part_a, held, total, *sems[5:7])
    gat_a = Gather(line, own_a, branch, *sems[7:10])
    red_b = Reduce(line, part_p, held, total, *sems[10:12])
    gat_b = Gather(line, own_p, mixed, *sems[12:15])
    dp_sems = sems[15:]
    upstream = cotangent
    gain = gain2

    def near_copy(c, src=cotangent):
        return pltpu.make_async_copy(src.at[gat_p.mine(c)], near.at[c], near_sem.at[c])

    def token_load(n):
        rows = slice(n * wide, (n + 1) * wide)
        return pltpu.make_async_copy(tokens.at[rows], hid.at[n % 2], in_sem.at[n % 2, 0])

    def hidden_save(n):
        rows = slice(n * wide, (n + 1) * wide)
        return pltpu.make_async_copy(dy.at[n % 2], hidden1.at[rows], save_sem.at[n % 2])

    def load(n):
        slot = n % 2
        rows = slice(n * wide, (n + 1) * wide)
        return (
            pltpu.make_async_copy(hidden2.at[rows], hid.at[slot], in_sem.at[slot, 0]),
            pltpu.make_async_copy(cotangent.at[rows], dy.at[slot], in_sem.at[slot, 1]),
        )

    weights = [
        pltpu.make_async_copy(src, dst, w_sem.at[i])
        for i, (src, dst) in enumerate(
            (
                (query_weight, wu.at[:, :lanes]),
                (kv_weight, wu.at[:, lanes : lanes + 2 * HD]),
                (out_weight, wd.at[:lanes]),
                (gate_weight, wg),
                (up_weight, wu),
                (down_weight, wd),
            )
        )
    ]
    token_load(0).start()
    for copy in weights[:4]:
        copy.start()
    for c in range(chunks):
        near_copy(c, tokens).start()
    line.greet(dps)
    grad_gain[...] = jnp.zeros_like(grad_gain)

    def project(n):
        rows = slice(n * wide, (n + 1) * wide)
        token_load(n).wait()
        if n + 1 < big:
            token_load(n + 1).start()
        if n >= 2:
            hidden_save(n - 2).wait()
        if n == 0:
            weights[0].wait()
            weights[1].wait()
        vector = hid[n % 2].astype(F32)
        hidden = (vector * normed(vector) * gain1[...]).astype(BF)
        dy[n % 2] = hidden
        hidden_save(n).start()
        cos, sin = cosine[:, rows], sine[:, rows]
        raw = nn(hidden, wu[:, :lanes]).T
        for h in range(heads):
            here = slice(h * HD, (h + 1) * HD)
            turned = rope(raw[here], cos, sin) * (HD ** (-0.5))
            query_t[here, rows] = turned.astype(BF)
        raw = nn(hidden, wu[:, lanes : lanes + 2 * HD]).T
        turned = rope(raw[:HD], cos, sin)
        keys_t[:, rows] = turned.astype(BF)
        keys[rows, :] = turned.T.astype(BF)
        values_t[:, rows] = raw[HD:].astype(BF)
        values[rows, :] = raw[HD:].T.astype(BF)

    def attend(n, begin, end):
        keys_n = (n + 1) * wide
        cols = slice(n * wide, keys_n)
        if begin == 0:
            bias[:keys_n, :] = visible_bias(seg_row[...], seg_key[...], n, wide)

        def head(h, carry):
            here = pl.ds(pl.multiple_of(h * HD, HD), HD)
            scores = nn(keys[:keys_n, :], query_t[here, cols]) + bias[:keys_n, :]
            peak = jnp.max(scores, axis=0, keepdims=True)
            weights = jnp.exp(scores - peak)
            sums = jnp.sum(weights, axis=0, keepdims=True)
            probs = (weights * (1.0 / sums)).astype(BF)
            heads_t[here, :] = nn(values_t[:, :keys_n], probs)
            logs[h, :, cols] = peak + jnp.log(sums)
            return carry

        lax.fori_loop(begin, end, head, 0)

    def close_heads(n):
        if n == 0:
            weights[2].wait()
        heads_n = heads_t[...].T.astype(BF)
        heads_out[n * wide : (n + 1) * wide, :] = heads_n
        step = min(512, width)
        for at in range(0, width, step):
            cols = slice(at, at + step)
            put(part_p, n, cols, nn(heads_n, wd[:lanes, cols]))
        if n == big - 1:
            weights[4].start()
            weights[5].start()

    def attn_tasks(n):
        return [
            functools.partial(project, n),
            functools.partial(attend, n, 0, heads // 2),
            functools.partial(attend, n, heads // 2, heads),
            functools.partial(close_heads, n),
        ]

    def norm(c):
        near_copy(c, tokens).wait()
        vector = near[c].astype(F32) + total[...]
        near_copy(c).start()
        resid[c] = vector
        own_p[c] = (vector * normed(vector) * gain2[...]).astype(BF)

    def saves(n):
        slot = n % 2
        rows = slice(n * wide, (n + 1) * wide)
        return [
            pltpu.make_async_copy(src.at[slot], dst.at[rows], out_sem.at[slot, i])
            for i, (src, dst) in enumerate(((act_c, active), (gate_c, grad_gate), (up_c, grad_up)))
        ]

    def enter(n):
        if n == 0:
            for k in range(max(0, big - 2), big):
                hidden_save(k).wait()
        for c in range(n * sub, (n + 1) * sub):
            gat_p.complete(c)
        for copy in load(n):
            copy.start()
        for c in range(n * sub, (n + 1) * sub):
            red_p.close(c)
            gat_p.close(c)
        for copy in load(n):
            copy.wait()
        if n == 0:
            for copy in weights[3:]:
                copy.wait()
        if n >= 2:
            for copy in saves(n - 2):
                copy.wait()
        slot = n % 2
        dy[slot] = jnp.where(live[n * wide : (n + 1) * wide, :] > 0, dy[slot], BF(0))

    def hidden_units(n, cols):
        slot = n % 2
        gate = nn(hid[slot], wg[:, cols])
        up = nn(hid[slot], wu[:, cols])
        grad = nt(dy[slot], wd[cols, :])
        sig = 1.0 / (1.0 + jnp.exp(-gate))
        silu = gate * sig
        act_c[slot, :, cols] = (silu * up).astype(BF)
        gate_c[slot, :, cols] = (grad * up * sig * (1.0 + gate * (1.0 - sig))).astype(BF)
        up_c[slot, :, cols] = (grad * silu).astype(BF)
        if cols.stop == units:
            for copy in saves(n):
                copy.start()

    def back_part(n, cols):
        slot = n % 2
        put(part_a, n, cols, nt(gate_c[slot], wg[cols, :]) + nt(up_c[slot], wu[cols, :]))

    def down_part(n, cols):
        put(part_p, n, cols, nn(act_c[n % 2], wd[:, cols]))

    def feed_tasks(n):
        step = 512
        unit_cols = [slice(at, min(at + step, units)) for at in range(0, units, step)]
        cols = [slice(at, at + step) for at in range(0, width, step)]

        def first():
            enter(n)
            hidden_units(n, unit_cols[0])

        def several(f, group):
            for here in group:
                f(n, here)

        return [
            first,
            *[functools.partial(hidden_units, n, here) for here in unit_cols[1:]],
            functools.partial(several, back_part, cols[:2]),
            functools.partial(several, back_part, cols[2:]),
            functools.partial(several, down_part, cols),
        ]

    spreads = [
        Spread(line, gate_stage, gate_out, gate_taken, gate_sums, gate_moved, dp_sems[:5]),
        Spread(line, up_stage, up_out, up_taken, up_sums, up_moved, dp_sems[5:10]),
        Spread(line, down_stage, down_out, down_taken, down_sums, down_moved, dp_sems[10:]),
    ]
    pair = 2 * width // dps
    groups = dps // 2
    turns = [
        pltpu.make_async_copy(src, dst, turn_sem.at[i])
        for i, (src, dst) in enumerate(
            (
                (grad_gate, wg.at[:length]),
                (grad_up, wg.at[length : 2 * length]),
                (active, wu.at[:length]),
            )
        )
    ]

    def pair_load(j, slot):
        cols = pl.ds(pl.multiple_of(line.group(j) * pair, pair), pair)
        at = 2 * slot * pair
        return (
            pltpu.make_async_copy(
                hidden2.at[:, cols], wd.at[:length, at : at + pair], pair_sem.at[slot, 0]
            ),
            pltpu.make_async_copy(
                upstream.at[:, cols],
                wd.at[:length, at + pair : at + 2 * pair],
                pair_sem.at[slot, 1],
            ),
        )

    units_order = list(range(1, groups)) + [0]

    def turn():
        for n in range(max(0, big - 2), big):
            for copy in saves(n):
                copy.wait()
        for copy in turns:
            copy.start()
        for copy in pair_load(units_order[0], 0):
            copy.start()

    def unit_enter(n):
        slot = n % 2
        for copy in pair_load(units_order[n], slot):
            copy.wait()
        if n == 0:
            for copy in turns:
                copy.wait()
            wu[:length, :] = jnp.where(live[...] > 0, wu[:length, :], BF(0))
        if n + 1 < groups:
            for copy in pair_load(units_order[n + 1], 1 - slot):
                copy.start()

    def unit_gate(n):
        at = 2 * (n % 2) * pair
        unit_enter(n)
        halves(gate_stage, tn(wd[:length, at : at + pair], wg[:length, :]), 0)
        spreads[0].give(units_order[n]).start()

    def unit_up(n):
        at = 2 * (n % 2) * pair
        halves(up_stage, tn(wd[:length, at : at + pair], wg[length : 2 * length, :]), 0)
        spreads[1].give(units_order[n]).start()

    def unit_down(n):
        at = 2 * (n % 2) * pair + pair
        halves(down_stage, tn(wu[:length, :], wd[:length, at : at + pair]), 1)
        spreads[2].give(units_order[n]).start()

    after = []
    for n in range(groups):
        for task in (unit_gate, unit_up, unit_down):
            after.append(functools.partial(task, n))
        after += merged(spreads, units_order[n])

    def done_a(c):
        near_copy(c).wait()
        grad = total[...]
        vector = resid[c]
        scale = normed(vector)
        scaled = grad * gain[...]
        inner = jnp.mean(scaled * vector, axis=-1, keepdims=True)
        grad_gain[...] += jnp.sum(grad * vector * scale, axis=0, keepdims=True)
        seen = live[gat_a.mine(c), :] > 0
        back = jnp.where(seen, near[c].astype(F32), 0.0)
        back = back + scale * scaled - vector * (scale * scale * scale) * inner
        grad_resid[c] = back
        own_a[c] = back.astype(BF)

    def done_b(c):
        own_p[c] = (resid[c] + total[...]).astype(BF)

    slots = [(red_p, gat_p, norm, c) for c in range(chunks)]
    slots += [(red_a, gat_a, done_a, c) for c in range(chunks)]
    slots += [(red_b, gat_b, done_b, c) for c in range(chunks)]
    plan = {}
    for n in range(1, big):
        schedule(plan, attn_tasks(n), sub * (n - 1), 4 // sub)
    for n in range(big):
        schedule(plan, feed_tasks(n), sub * (big - 1 + n), 6 // sub)
    schedule(plan, [turn], sub * (2 * big - 1), 1)
    schedule(plan, after, sub * (2 * big - 1), 4)

    def begin(i):
        if i == 0:
            for task in attn_tasks(0):
                task()
        if i < len(slots):
            red, _, _, c = slots[i]
            red.start(c)

    drive(slots, begin, plan)
    for i in sorted(plan):
        if i >= len(slots) + 4:
            for task in plan[i]:
                task()
    finished(spreads)
    for red, gat, done, c in slots[chunks:]:
        red.close(c)
        gat.complete(c)
        gat.close(c)


def back_kernel(
    chunks,
    big,
    dps,
    branch,
    tokens,
    resid_in,
    gain,
    seg_row,
    seg_key,
    cosine,
    sine,
    query_t,
    keys,
    keys_t,
    values,
    logs,
    out_weight,
    query_in,
    kv_weight,
    other_gain,
    heads_in,
    hidden1,
    tokens_grad,
    gains_out,
    out_out,
    qkv_out,
    out_taken,
    out_sums,
    out_moved,
    qkv_taken,
    qkv_sums,
    qkv_moved,
    grad_resid,
    query_weight,
    heads_out,
    grad_gain,
    gain_parts,
    gain_dp,
    gain_sum,
    gain_z,
    grad_qkv,
    out_stage,
    qkv_stage,
    pair_out,
    pair_qkv,
    bias,
    dy,
    do_t,
    do_h,
    dq_t,
    dk,
    dv,
    part,
    held,
    total,
    own,
    near,
    in_sem,
    tok_sem,
    red_send,
    red_recv,
    gat_send,
    gat_recv,
    gat_stay,
    pair_sem,
    late_sem,
    gain_send,
    gain_recv,
    zsum_send,
    zsum_recv,
    *dp_sems,
):
    length, width = tokens.shape
    chunk = length // chunks
    wide = length // big
    sub = chunks // big
    piece = chunk // 4
    heads = query_t.shape[0] // HD
    factor = HD ** (-0.5)
    line = Line(piece)
    red = Reduce(line, part, held, total, red_send, red_recv)
    gat = Gather(line, own, tokens_grad, gat_send, gat_recv, gat_stay)
    order = list(reversed(range(big)))

    def load(c, slot):
        return pltpu.make_async_copy(
            branch.at[c * wide : (c + 1) * wide], dy.at[slot], in_sem.at[slot]
        )

    def near_copy(c):
        return pltpu.make_async_copy(tokens.at[gat.mine(c)], near.at[c], tok_sem.at[c])

    load(order[0], 0).start()
    for c in range(chunks):
        near_copy(c).start()
    late = [
        pltpu.make_async_copy(src, dst, late_sem.at[i])
        for i, (src, dst) in enumerate(
            ((query_in, query_weight), (resid_in, grad_resid), (heads_in, heads_out))
        )
    ]
    for copy in late:
        copy.start()
    line.greet(dps, every=True)
    grad_gain[...] = jnp.zeros_like(grad_gain)
    dk[...] = jnp.zeros_like(dk)
    dv[...] = jnp.zeros_like(dv)

    def enter(i):
        c, slot = order[i], i % 2
        load(c, slot).wait()
        if i + 1 < big:
            load(order[i + 1], 1 - slot).start()
        keys_n = (c + 1) * wide
        bias[:keys_n, :] = visible_bias(seg_row[...], seg_key[...], c, wide)
        grad_heads = nt(dy[slot], out_weight[...])
        do_t[...] = grad_heads.T.astype(BF)
        for h in range(heads):
            do_h[h] = grad_heads[:, h * HD : (h + 1) * HD].astype(BF)

    def attend(i, begin, end):
        c = order[i]
        keys_n = (c + 1) * wide
        cols = slice(c * wide, keys_n)

        def head(h, carry):
            here = pl.ds(pl.multiple_of(h * HD, HD), HD)
            scores = nn(keys[:keys_n, :], query_t[here, cols]) + bias[:keys_n, :]
            probs = jnp.exp(scores - logs[h, :, cols])
            grad_probs = nn(values[:keys_n, :], do_t[here, :])
            delta = jnp.sum(probs * grad_probs, axis=0, keepdims=True)
            grad_scores = (probs * (grad_probs - delta)).astype(BF)
            dv[:keys_n, :] += nn(probs.astype(BF), do_h[h])
            dk[:keys_n, :] += nn(grad_scores, query_t[here, cols].T)
            grad = nn(keys_t[:, :keys_n], grad_scores) * factor
            dq_t[here, :] = unrope(grad, cosine[:, cols], sine[:, cols])
            return carry

        lax.fori_loop(begin, end, head, 0)

    def leave(i):
        c = order[i]
        cols = slice(c * wide, (c + 1) * wide)
        lanes = heads * HD
        grad_qkv[cols, :lanes] = dq_t[...].T.astype(BF)
        grad_k = unrope(dk[cols, :].T, cosine[:, cols], sine[:, cols]).T
        grad_qkv[cols, lanes:] = jnp.concatenate([grad_k, dv[cols, :]], axis=1).astype(BF)
        if i == 0:
            for copy in late:
                copy.wait()
        step = min(512, width)
        for n in range(0, width, step):
            here = slice(n, n + step)
            value = nt(grad_qkv[cols, :lanes], query_weight[here, :])
            put(part, c, here, value + nt(grad_qkv[cols, lanes:], kv_weight[here, :]))

    def tasks(i):
        half = heads // 2
        return [
            functools.partial(enter, i),
            functools.partial(attend, i, 0, half),
            functools.partial(attend, i, half, heads),
            functools.partial(leave, i),
        ]

    spread_out = Spread(line, out_stage, out_out, out_taken, out_sums, out_moved, dp_sems[:5])
    spread_qkv = Spread(line, qkv_stage, qkv_out, qkv_taken, qkv_sums, qkv_moved, dp_sems[5:])
    pair = 2 * width // dps
    groups = dps // 2
    units_order = list(range(1, groups)) + [0]

    def pair_load(j, slot, src, dst, number):
        cols = pl.ds(pl.multiple_of(line.group(j) * pair, pair), pair)
        return pltpu.make_async_copy(src.at[:, cols], dst.at[slot], pair_sem.at[slot, number])

    def unit_out(n):
        j, slot = units_order[n], n % 2
        pair_load(j, slot, branch, pair_out, 0).wait()
        if n + 1 < groups:
            pair_load(units_order[n + 1], 1 - slot, branch, pair_out, 0).start()
        halves(out_stage, tn(heads_out[...], pair_out[slot]), 1)
        spread_out.give(j).start()

    def unit_qkv(n):
        j, slot = units_order[n], n % 2
        pair_load(j, slot, hidden1, pair_qkv, 1).wait()
        if n + 1 < groups:
            pair_load(units_order[n + 1], 1 - slot, hidden1, pair_qkv, 1).start()
        halves(qkv_stage, tn(pair_qkv[slot], grad_qkv[...]), 0)
        spread_qkv.give(j).start()

    pair_load(units_order[0], 0, branch, pair_out, 0).start()
    pair_load(units_order[0], 0, hidden1, pair_qkv, 1).start()
    work_out, work_qkv = [], []
    for n in range(groups):
        work_out.append(functools.partial(unit_out, n))
        work_out += merged([spread_out], units_order[n])
        work_qkv.append(functools.partial(unit_qkv, n))
        work_qkv += merged([spread_qkv], units_order[n])

    def done(c):
        near_copy(c).wait()
        grad = total[...]
        vector = near[c].astype(F32)
        scale = normed(vector)
        scaled = grad * gain[...]
        inner = jnp.mean(scaled * vector, axis=-1, keepdims=True)
        grad_gain[...] += jnp.sum(grad * vector * scale, axis=0, keepdims=True)
        back = grad_resid[c] + scale * scaled - vector * (scale * scale * scale) * inner
        own[c] = back.astype(BF)

    block = width // dps
    slots = [(red, gat, done, c) for c in reversed(range(chunks))]

    def gain_move(j):
        return pltpu.make_async_remote_copy(
            src_ref=gain_parts.at[line.dp_peer(j)],
            dst_ref=gain_dp.at[j],
            send_sem=gain_send.at[j],
            recv_sem=gain_recv.at[j],
            device_id=(line.dp_peer(j), line.z),
            device_id_type=MESH,
        )

    def gain_share(j):
        return pltpu.make_async_remote_copy(
            src_ref=gain_sum,
            dst_ref=gain_z.at[j],
            send_sem=zsum_send.at[j],
            recv_sem=zsum_recv.at[j],
            device_id=(line.dp, line.z_peer(j)),
            device_id_type=MESH,
        )

    def gains_dp():
        both = jnp.concatenate([grad_gain[...], other_gain[...]], axis=0)
        for d in range(dps):
            gain_parts[d] = both[:, d * block : (d + 1) * block]
        for j in range(1, dps):
            gain_move(j).start()

    def gains_line():
        for j in range(1, dps):
            gain_move(j).wait()
        value = gain_parts[line.dp]
        for j in range(1, dps):
            value = value + gain_dp[j]
        gain_sum[...] = value
        for j in range(1, 4):
            gain_share(j).start()

    def gains_end():
        value = gain_sum[...]
        for j in range(1, 4):
            gain_share(j).wait()
            value = value + gain_z[j]
        gains_out[...] = value

    plan = {}
    for i in range(1, big):
        schedule(plan, tasks(i), sub * (i - 1), 4 // sub)
    schedule(plan, work_out, 1, 3)
    schedule(plan, work_qkv, sub * (big - 1), 4)

    def begin(i):
        if i == 0:
            for task in tasks(0):
                task()
        if i < chunks:
            red.start(slots[i][3])
        if i == chunks + 2:
            gains_dp()
        if i == chunks + 3:
            gains_line()

    drive(slots, begin, plan)
    for i in sorted(plan):
        if i >= chunks + 4:
            for task in plan[i]:
                task()
    gains_end()
    finished([spread_out, spread_qkv])
    for red, gat, done, c in slots:
        red.close(c)
        gat.complete(c)
        gat.close(c)


def call(kernel, ins, outs, scratch, number, cost):
    return pl.pallas_call(
        kernel,
        in_specs=[spec for spec, _ in ins],
        out_specs=[spec for spec, _, _ in outs],
        out_shape=[jax.ShapeDtypeStruct(shape, kind) for _, shape, kind in outs],
        scratch_shapes=scratch,
        compiler_params=pltpu.CompilerParams(
            collective_id=number, has_side_effects=True, vmem_limit_bytes=LIMIT
        ),
        cost_estimate=pl.CostEstimate(flops=cost, bytes_accessed=cost // 1000, transcendentals=0),
    )(*[array for _, array in ins])


def line_scratch(chunks, piece, width):
    dma = pltpu.SemaphoreType.DMA
    buffers = [
        pltpu.VMEM((chunks, 4 * piece, width), BF),
        pltpu.VMEM((DEPTH, 5, piece, width), BF),
        pltpu.VMEM((chunks, piece, width), BF),
    ]
    sems = [dma((chunks, 3)), dma((chunks, 5)), dma((chunks, 5)), dma((chunks, 4)), dma((chunks,))]
    return buffers, sems


def spread_shapes(groups, rows, cols):
    dma = pltpu.SemaphoreType.DMA
    outs = [(VMEM, (rows, cols), F32)]
    boxes = [(ANY, (groups, rows, cols), BF)] * 3
    stage = pltpu.VMEM((2, rows, cols), BF)
    return outs, boxes, stage, [dma((groups,))] * 4 + [dma((2,))]


def tables(seg_row):
    length = seg_row.shape[0]
    start = jnp.sum((seg_row[None, :] < seg_row[:, None]).astype(jnp.int32), axis=1)
    place = (jnp.arange(length, dtype=jnp.int32) - start).astype(F32)
    half = HD // 2
    freq = jnp.power(jnp.float32(THETA), -jnp.arange(half, dtype=F32) / half)
    angle = freq[:, None] * place[None, :]
    return jnp.cos(angle), jnp.sin(angle)


def local(
    dps,
    tokens,
    segments,
    counts,
    cotangent,
    attn_gain,
    mlp_gain,
    query_weight,
    key_weight,
    value_weight,
    out_weight,
    gate_weight,
    up_weight,
    down_weight,
):
    length, width = tokens.shape
    units = gate_weight.shape[1]
    lanes = query_weight.shape[1]
    heads = lanes // HD
    chunks, big = CHUNKS, BIG
    chunk = length // chunks
    wide = length // big
    piece = chunk // 4
    dma = pltpu.SemaphoreType.DMA
    groups = dps // 2
    block = width // dps

    live = jnp.arange(length, dtype=jnp.int32) < counts[0]
    seg_row = segments.reshape(1, length)
    seg_key = jnp.where(live, segments, -1).reshape(length, 1)
    live = live.astype(jnp.int32).reshape(length, 1)
    cosine, sine = tables(segments)
    gain1 = attn_gain.reshape(1, width)
    gain2 = mlp_gain.reshape(1, width)

    buffers, sems = line_scratch(chunks, piece, width)
    total = pltpu.VMEM((piece, width), F32)
    near = pltpu.VMEM((chunks, piece, width), BF)
    by_rows = spread_shapes(groups, block, units)
    by_cols = spread_shapes(groups, units, block)
    kv_weight = jnp.concatenate([key_weight, value_weight], axis=1)
    (
        mixed,
        branch,
        hidden1,
        grad_resid,
        grad_gain2,
        heads_out,
        logs,
        query_t,
        keys,
        keys_t,
        values,
        gate_grad,
        up_grad,
        down_grad,
        *_,
    ) = call(
        functools.partial(front_kernel, chunks, big, dps),
        [
            (ANY, tokens),
            (ANY, cotangent),
            (VMEM, live),
            (VMEM, gain1),
            (VMEM, gain2),
            (VMEM, seg_row),
            (VMEM, seg_key),
            (VMEM, cosine),
            (VMEM, sine),
            (ANY, query_weight),
            (ANY, kv_weight),
            (ANY, out_weight),
            (ANY, gate_weight),
            (ANY, up_weight),
            (ANY, down_weight),
        ],
        [
            (ANY, (length, width), BF),
            (ANY, (length, width), BF),
            (ANY, (length, width), BF),
            (VMEM, (chunks, piece, width), F32),
            (VMEM, (1, width), F32),
            (VMEM, (length, lanes), BF),
            (VMEM, (heads, 1, length), F32),
            (VMEM, (lanes, length), BF),
            (VMEM, (length, HD), BF),
            (VMEM, (HD, length), BF),
            (VMEM, (length, HD), BF),
            *by_rows[0],
            *by_rows[0],
            *by_cols[0],
            (ANY, (length, width), BF),
            *[(ANY, (length, units), BF)] * 3,
            *by_rows[1],
            *by_rows[1],
            *by_cols[1],
        ],
        [
            pltpu.VMEM((width, units), BF),
            pltpu.VMEM((width, units), BF),
            pltpu.VMEM((units, width), BF),
            pltpu.VMEM((2, wide, width), BF),
            pltpu.VMEM((2, wide, width), BF),
            pltpu.VMEM((2, wide, units), BF),
            pltpu.VMEM((2, wide, units), BF),
            pltpu.VMEM((2, wide, units), BF),
            *[pltpu.VMEM((2, 16, units), BF) if block == wide else by_rows[2]] * 2,
            by_cols[2],
            pltpu.VMEM((HD, length), BF),
            pltpu.VMEM((length, wide), F32),
            pltpu.VMEM((lanes, wide), F32),
            pltpu.VMEM((chunks, piece, width), F32),
            buffers[0],
            buffers[0],
            buffers[1],
            buffers[2],
            buffers[2],
            near,
            total,
            dma((6,)),
            dma((2, 2)),
            dma((2, 3)),
            dma((2,)),
            dma((chunks,)),
            dma((3,)),
            dma((2, 2)),
            *sems,
            *sems,
            *sems,
            *by_rows[3],
            *by_rows[3],
            *by_cols[3],
        ],
        0,
        5 * 10**10,
    )

    by_cols = spread_shapes(groups, lanes, block)
    by_rows = spread_shapes(groups, block, lanes + 2 * HD)
    tokens_grad, gains, out_grad, qkv_grad, *_ = call(
        functools.partial(back_kernel, chunks, big, dps),
        [
            (ANY, branch),
            (ANY, tokens),
            (ANY, grad_resid),
            (VMEM, gain1),
            (VMEM, seg_row),
            (VMEM, seg_key),
            (VMEM, cosine),
            (VMEM, sine),
            (VMEM, query_t),
            (VMEM, keys),
            (VMEM, keys_t),
            (VMEM, values),
            (VMEM, logs),
            (VMEM, out_weight),
            (ANY, query_weight),
            (VMEM, kv_weight),
            (VMEM, grad_gain2),
            (ANY, heads_out),
            (ANY, hidden1),
        ],
        [
            (ANY, (length, width), BF),
            (VMEM, (2, block), F32),
            *by_cols[0],
            *by_rows[0],
            *by_cols[1],
            *by_rows[1],
        ],
        [
            pltpu.VMEM((chunks, piece, width), F32),
            pltpu.VMEM((width, lanes), BF),
            pltpu.VMEM((length, lanes), BF),
            pltpu.VMEM((1, width), F32),
            pltpu.VMEM((dps, 2, block), F32),
            pltpu.VMEM((dps, 2, block), F32),
            pltpu.VMEM((2, block), F32),
            pltpu.VMEM((4, 2, block), F32),
            pltpu.VMEM((length, lanes + 2 * HD), BF),
            by_cols[2],
            by_rows[2],
            pltpu.VMEM((2, length, 2 * block), BF),
            pltpu.VMEM((2, length, 2 * block), BF),
            pltpu.VMEM((length, wide), F32),
            pltpu.VMEM((2, wide, width), BF),
            pltpu.VMEM((lanes, wide), BF),
            pltpu.VMEM((heads, wide, HD), BF),
            pltpu.VMEM((lanes, wide), F32),
            pltpu.VMEM((length, HD), F32),
            pltpu.VMEM((length, HD), F32),
            buffers[0],
            buffers[1],
            total,
            buffers[2],
            near,
            dma((2,)),
            dma((chunks,)),
            *sems,
            dma((2, 2)),
            dma((3,)),
            dma((dps,)),
            dma((dps,)),
            dma((4,)),
            dma((4,)),
            *by_cols[3],
            *by_rows[3],
        ],
        1,
        2 * 10**10,
    )

    return (
        mixed,
        tokens_grad,
        gains[0],
        gains[1],
        qkv_grad[:, :lanes],
        qkv_grad[:, lanes : lanes + HD],
        qkv_grad[:, lanes + HD :],
        out_grad,
        gate_grad,
        up_grad,
        down_grad,
    )


def solution(mesh):
    placed = (
        P("dp", None),
        P("dp"),
        P("dp"),
        P("dp", None),
        P(),
        P(),
        P(None, "tensor"),
        P(None, "tensor"),
        P(None, "tensor"),
        P("tensor", None),
        P(None, "tensor"),
        P(None, "tensor"),
        P("tensor", None),
    )
    return jax.shard_map(
        functools.partial(local, mesh.shape["dp"]),
        mesh=mesh,
        in_specs=placed,
        out_specs=(
            P("dp", None),
            P("dp", None),
            P("dp"),
            P("dp"),
            P("dp", "tensor"),
            P("dp", "tensor"),
            P("dp", "tensor"),
            P("tensor", "dp"),
            P("dp", "tensor"),
            P("dp", "tensor"),
            P("tensor", "dp"),
        ),
        check_vma=False,
    )
```

time: 694 us -> 490 us (0.71)
  Pallas kernels: 561 us -> 453 us
  waiting for transfers between devices: 34.6 us -> 0 us
  other arithmetic: 23.5 us -> 5.19 us
  between operations: 15.4 us -> 1.54 us
  local copies, waits for them, and re-layouts: 32 us -> 20.3 us
  blocking collectives: 11.7 us -> 0 us
  matrix products: 8.7 us -> 0 us
    pallas_call x3 -> x2, Pallas kernels: 561 us -> 453 us  [call(): pl.pallas_call(kernel, in_specs=[spec for spec, _ in ins], out_specs=[spe...]
    unnamed x2 -> x0, waiting for transfers between devices: 34.6 us -> none
    psum x1 -> x0, blocking collectives: 11.7 us -> none  [local(): lax.psum(jnp.concatenate([grad_gain1, grad_gain2], axis=0), 'tensor')]
    dot_general x3 -> x0, matrix products: 8.7 us -> none  [the longest x1 5.23 us: local(): lax.dot_general(query_weight, hidden1, dims, preferred_element_type=F32)]
    unnamed x48 -> x20, local copies, waits for them, and re-layouts: 21.1 us -> 15.1 us
  transfers between devices with their start and end apart: 1 -> 0, of which waited for: 1 -> 0; matrix products, arithmetic and copies ran while one was open for 1% -> 0% of each run, Pallas kernels for 0% -> 0%
where the time goes in v3:
time: 490 us; the launch traced here: 481 us
  Pallas kernels  453 us (92%)
  local copies, waits for them, and re-layouts  20.3 us (4%)
  other arithmetic  5.19 us (1%)
    pallas_call x2, Pallas kernels, call(): pl.pallas_call(kernel, in_specs=[spec for spec, _ in ins], out_specs=[spe...  453 us
    unnamed x20, local copies, waits for them, and re-layouts  15.1 us

profile of v3, /device:TPU:0, one launch (start us, length us, event | category | flops | bytes accessed | tf_op | source)
XLA Modules:
  0.0 480.5 jit_solution(16632772258488202693)
XLA Ops:
  1.3 0.7 fusion.1
  2.0 1.3 convert_reduce_fusion
  3.3 1.2 multiply_sine_fusion
  4.6 1.0 copy.36.seg_key
  5.6 1.2 copy.34
  6.8 1.2 copy.35
  8.1 1.1 pad_maximum_fusion.kv_weight
  9.1 0.8 fusion.live
  10.0 317.5 %shard_map.212 = (bf16[1024,2048]{1,0:T(8,128)(2,1)}, bf16[1024,2048]{1,0:T(8,128)(2,1)}, bf16[1024,2048]{1,0:T(8,128)(2,1)}, f32[8,32,2048]{2,1,0:T(8,128)}, f3...) custom-call(bf16[1024,2048]{1,0:T(8,128)(2,1)} %tokens.3, ...), custom_call_target="tpu_custom_call" | custom-call | flops 49999998976 | bytes 50000000 | tf_op jit(solution)/shard_map/pallas_call | solution.py:1144
  327.5 135.9 %shard_map.213 = (bf16[1024,2048]{1,0:T(8,128)(2,1)}, f32[2,256]{1,0:T(2,128)}, f32[512,256]{1,0:T(8,128)}, f32[256,640]{1,0:T(8,128)}, bf16[4,512,256]{2,1,0:T(...) custom-call(bf16[1024,2048]{1,0:T(8,128)(2,1)} %get-tuple-element.30, ...), custom_call_target="tpu_custom_call" | custom-call | flops 20000000000 | bytes 20000000 | tf_op jit(solution)/shard_map/pallas_call | solution.py:1144
  463.4 1.3 fusion.3
  464.7 1.1 fusion.2
  465.8 1.9 slice.17
  467.7 0.7 copy.39
  468.4 0.7 copy.38
  469.1 0.0 copy-start
  469.1 4.9 %copy.47 = bf16[1024,2048]{1,0:T(8,128)(2,1)} copy(bf16[1024,2048]{1,0:T(8,128)(2,1)} %get-tuple-element.97) | data formatting | bytes 8388608
  474.1 0.0 copy-done
  474.1 0.0 copy-start.4
  474.1 0.0 copy-start.3
  474.1 2.1 copy.48
  476.2 0.0 copy-done.4
  476.2 0.0 copy-start.2
  476.2 0.8 copy.49
  477.0 0.1 copy-done.3
  477.0 0.0 copy-start.1
  477.0 1.1 copy.50
  478.1 0.0 copy-done.2
  478.1 1.1 copy.51
  479.2 0.0 copy-done.1
  479.2 1.1 copy.52
  (2 shorter events, 0.0 us)
Async XLA Ops:
  469.1 4.9 %copy-start = (bf16[1024,2048]{1,0:T(8,128)(2,1)S(1)}, bf16[1024,2048]{1,0:T(8,128)(2,1)}, u32[]{:S(2)}) copy-start(bf16[1024,2048]{1,0:T(8,128)(2,1)} %get-tuple-element.98) | copy-start | bytes 12582916
  474.1 2.1 copy-start.4
  474.1 3.0 copy-start.3
  476.2 2.0 copy-start.2
  477.0 2.2 copy-start.1

commit v4 on v3

--- a/solution.py
+++ b/solution.py
@@ -19,7 +19,7 @@
 F32 = jnp.float32
 ANY = pl.BlockSpec(memory_space=pl.ANY)
 VMEM = pl.BlockSpec(memory_space=pltpu.VMEM)
-LIMIT = 60 * 1024 * 1024
+LIMIT = 62 * 1024 * 1024
 
 
 def nn(a, b):
@@ -107,15 +107,19 @@
 
 
 class Reduce:
-    def __init__(self, line, part, held, total, send, recv):
+    def __init__(self, line, part, held, total, send, recv, last=None):
+        self.last = last
         self.line, self.part, self.held, self.total = line, part, held, total
         self.send, self.recv = send, recv
+
+    def place(self, c):
+        return (c if self.last is None else self.last - c) % DEPTH
 
     def copy(self, c, m, slot, target, number):
         line = self.line
         return line.copy(
             self.part.at[c, line.at(m)],
-            self.held.at[c % DEPTH, slot],
+            self.held.at[self.place(c), slot],
             self.send.at[c, number],
             self.recv.at[c, slot],
             target,
@@ -138,7 +142,7 @@
             self.arrived(c, m - 1)
             rows = line.at(m)
             self.part[c, rows] = (
-                self.part[c, rows].astype(F32) + self.held[c % DEPTH, m - 1].astype(F32)
+                self.part[c, rows].astype(F32) + self.held[self.place(c), m - 1].astype(F32)
             ).astype(BF)
             self.copy(c, m, 6 - m, line.inner, 3 - m).start()
 
@@ -150,7 +154,7 @@
             self.arrived(c, 3)
             rows = line.at(0)
             self.part[c, rows] = (
-                self.part[c, rows].astype(F32) + self.held[c % DEPTH, 3].astype(F32)
+                self.part[c, rows].astype(F32) + self.held[self.place(c), 3].astype(F32)
             ).astype(BF)
             self.copy(c, 0, 3, line.outer, 2).start()
 
@@ -160,7 +164,7 @@
         @pl.when(line.end)
         def _():
             self.arrived(c, 3)
-            self.total[...] = self.part[c, line.at(0)].astype(F32) + self.held[c % DEPTH, 3].astype(F32)
+            self.total[...] = self.part[c, line.at(0)].astype(F32) + self.held[self.place(c), 3].astype(F32)
 
         @pl.when(line.mid)
         def _():
@@ -168,8 +172,8 @@
             self.arrived(c, 4)
             self.total[...] = (
                 self.part[c, line.at(1)].astype(F32)
-                + self.held[c % DEPTH, 0].astype(F32)
-                + self.held[c % DEPTH, 4].astype(F32)
+                + self.held[self.place(c), 0].astype(F32)
+                + self.held[self.place(c), 4].astype(F32)
             )
 
     def close(self, c):
@@ -178,8 +182,8 @@
 
 
 class Spread:
-    def __init__(self, line, stage, out, taken, sums, moved, sems):
-        self.line, self.stage, self.out = line, stage, out
+    def __init__(self, line, stage, acc, taken, sums, moved, sems):
+        self.line, self.stage, self.acc = line, stage, acc
         self.taken, self.sums, self.moved = taken, sums, moved
         self.send1, self.recv1, self.send2, self.recv2, self.stay = sems
 
@@ -241,9 +245,9 @@
             self.load(source, j % 2).wait()
             block = self.stage[j % 2].astype(F32)
             if j:
-                self.out[...] += block
+                self.acc[...] += block
             else:
-                self.out[...] = block
+                self.acc[...] = block
 
 
 def merged(spreads, j):
@@ -254,11 +258,16 @@
     return [functools.partial(run, name) for name in ("merge_load", "merge_add", "merge_move")]
 
 
-def finished(spreads):
-    for spread in spreads:
+def finished(spread, copies, before=()):
+    def run():
         spread.last_load()
-    for spread in spreads:
+        for copy in before:
+            copy.wait()
         spread.last()
+        for copy in copies:
+            copy.start()
+
+    return run
 
 
 def halves(stage, value, dim):
@@ -442,7 +451,7 @@
     return jnp.where(seen, 0.0, NEGATIVE)
 
 
-def front_kernel(
+def layer_kernel(
     chunks,
     big,
     dps,
@@ -462,19 +471,17 @@
     up_weight,
     down_weight,
     mixed,
-    branch,
-    hidden1,
-    grad_resid,
-    grad_gain,
-    heads_out,
-    logs,
-    query_t,
-    keys,
-    keys_t,
-    values,
+    tokens_grad,
+    gains_out,
+    query_out,
+    key_out,
+    value_out,
+    out_out,
     gate_out,
     up_out,
     down_out,
+    branch,
+    hidden1,
     hidden2,
     active,
     grad_gate,
@@ -488,6 +495,12 @@
     down_taken,
     down_sums,
     down_moved,
+    out_taken,
+    out_sums,
+    out_moved,
+    qkv_taken,
+    qkv_sums,
+    qkv_moved,
     wg,
     wu,
     wd,
@@ -499,6 +512,28 @@
     gate_stage,
     up_stage,
     down_stage,
+    out_stage,
+    qkv_stage,
+    rows_acc,
+    cols_acc,
+    out_acc,
+    qkv_acc,
+    heads_out,
+    logs,
+    query_t,
+    keys,
+    keys_t,
+    values,
+    do_t,
+    dk,
+    dv,
+    grad_resid,
+    grad_gain1,
+    grad_gain2,
+    gain_parts,
+    gain_dp,
+    gain_sum,
+    gain_z,
     values_t,
     bias,
     heads_t,
@@ -517,6 +552,12 @@
     near_sem,
     turn_sem,
     pair_sem,
+    late_sem,
+    exit_sem,
+    gain_send,
+    gain_recv,
+    zsum_send,
+    zsum_recv,
     *sems,
 ):
     length, width = tokens.shape
@@ -536,9 +577,10 @@
     gat_a = Gather(line, own_a, branch, *sems[7:10])
     red_b = Reduce(line, part_p, held, total, *sems[10:12])
     gat_b = Gather(line, own_p, mixed, *sems[12:15])
-    dp_sems = sems[15:]
-    upstream = cotangent
-    gain = gain2
+    red_q = Reduce(line, part_a, held, total, *sems[15:17], last=chunks - 1)
+    gat_q = Gather(line, own_a, tokens_grad, *sems[17:20])
+    dp_sems = sems[20:]
+    factor = HD ** (-0.5)
 
     def near_copy(c, src=cotangent):
         return pltpu.make_async_copy(src.at[gat_p.mine(c)], near.at[c], near_sem.at[c])
@@ -577,8 +619,9 @@
         copy.start()
     for c in range(chunks):
         near_copy(c, tokens).start()
-    line.greet(dps)
-    grad_gain[...] = jnp.zeros_like(grad_gain)
+    line.greet(dps, every=True)
+    for zero in (grad_gain1, grad_gain2, dk, dv):
+        zero[...] = jnp.zeros_like(zero)
 
     def project(n):
         rows = slice(n * wide, (n + 1) * wide)
@@ -727,10 +770,12 @@
         ]
 
     spreads = [
-        Spread(line, gate_stage, gate_out, gate_taken, gate_sums, gate_moved, dp_sems[:5]),
-        Spread(line, up_stage, up_out, up_taken, up_sums, up_moved, dp_sems[5:10]),
-        Spread(line, down_stage, down_out, down_taken, down_sums, down_moved, dp_sems[10:]),
+        Spread(line, gate_stage, rows_acc, gate_taken, gate_sums, gate_moved, dp_sems[:5]),
+        Spread(line, up_stage, rows_acc, up_taken, up_sums, up_moved, dp_sems[5:10]),
+        Spread(line, down_stage, cols_acc, down_taken, down_sums, down_moved, dp_sems[10:15]),
     ]
+    spread_out = Spread(line, out_stage, out_acc, out_taken, out_sums, out_moved, dp_sems[15:20])
+    spread_qkv = Spread(line, qkv_stage, qkv_acc, qkv_taken, qkv_sums, qkv_moved, dp_sems[20:])
     pair = 2 * width // dps
     groups = dps // 2
     turns = [
@@ -744,6 +789,29 @@
         )
     ]
 
+    half_lanes = lanes // 2
+    kv = 2 * HD
+    late = [
+        pltpu.make_async_copy(src, dst, late_sem.at[i])
+        for i, (src, dst) in enumerate(
+            [(out_weight.at[k * wide : (k + 1) * wide], dy.at[k]) for k in range(2)]
+            + [
+                (
+                    query_weight.at[k * length : (k + 1) * length],
+                    wu.at[length : 2 * length, k * lanes : (k + 1) * lanes],
+                )
+                for k in range(2)
+            ]
+            + [
+                (
+                    kv_weight.at[k * length : (k + 1) * length],
+                    wu.at[length : 2 * length, 2 * lanes + k * kv : 2 * lanes + (k + 1) * kv],
+                )
+                for k in range(2)
+            ]
+        )
+    ]
+
     def pair_load(j, slot):
         cols = pl.ds(pl.multiple_of(line.group(j) * pair, pair), pair)
         at = 2 * slot * pair
@@ -752,7 +820,7 @@
                 hidden2.at[:, cols], wd.at[:length, at : at + pair], pair_sem.at[slot, 0]
             ),
             pltpu.make_async_copy(
-                upstream.at[:, cols],
+                cotangent.at[:, cols],
                 wd.at[:length, at + pair : at + 2 * pair],
                 pair_sem.at[slot, 1],
             ),
@@ -764,7 +832,7 @@
         for n in range(max(0, big - 2), big):
             for copy in saves(n):
                 copy.wait()
-        for copy in turns:
+        for copy in turns + late:
             copy.start()
         for copy in pair_load(units_order[0], 0):
             copy.start()
@@ -808,171 +876,46 @@
         grad = total[...]
         vector = resid[c]
         scale = normed(vector)
-        scaled = grad * gain[...]
+        scaled = grad * gain2[...]
         inner = jnp.mean(scaled * vector, axis=-1, keepdims=True)
-        grad_gain[...] += jnp.sum(grad * vector * scale, axis=0, keepdims=True)
+        grad_gain2[...] += jnp.sum(grad * vector * scale, axis=0, keepdims=True)
         seen = live[gat_a.mine(c), :] > 0
         back = jnp.where(seen, near[c].astype(F32), 0.0)
         back = back + scale * scaled - vector * (scale * scale * scale) * inner
         grad_resid[c] = back
         own_a[c] = back.astype(BF)
+        near_copy(c, tokens).start()
 
     def done_b(c):
         own_p[c] = (resid[c] + total[...]).astype(BF)
 
-    slots = [(red_p, gat_p, norm, c) for c in range(chunks)]
-    slots += [(red_a, gat_a, done_a, c) for c in range(chunks)]
-    slots += [(red_b, gat_b, done_b, c) for c in range(chunks)]
-    plan = {}
-    for n in range(1, big):
-        schedule(plan, attn_tasks(n), sub * (n - 1), 4 // sub)
-    for n in range(big):
-        schedule(plan, feed_tasks(n), sub * (big - 1 + n), 6 // sub)
-    schedule(plan, [turn], sub * (2 * big - 1), 1)
-    schedule(plan, after, sub * (2 * big - 1), 4)
-
-    def begin(i):
+    order = list(reversed(range(big)))
+
+    def branch_load(c, slot):
+        return pltpu.make_async_copy(
+            branch.at[c * wide : (c + 1) * wide], hid.at[slot], in_sem.at[slot, 0]
+        )
+
+    def back_enter(i):
+        c, slot = order[i], i % 2
         if i == 0:
-            for task in attn_tasks(0):
-                task()
-        if i < len(slots):
-            red, _, _, c = slots[i]
-            red.start(c)
-
-    drive(slots, begin, plan)
-    for i in sorted(plan):
-        if i >= len(slots) + 4:
-            for task in plan[i]:
-                task()
-    finished(spreads)
-    for red, gat, done, c in slots[chunks:]:
-        red.close(c)
-        gat.complete(c)
-        gat.close(c)
-
-
-def back_kernel(
-    chunks,
-    big,
-    dps,
-    branch,
-    tokens,
-    resid_in,
-    gain,
-    seg_row,
-    seg_key,
-    cosine,
-    sine,
-    query_t,
-    keys,
-    keys_t,
-    values,
-    logs,
-    out_weight,
-    query_in,
-    kv_weight,
-    other_gain,
-    heads_in,
-    hidden1,
-    tokens_grad,
-    gains_out,
-    out_out,
-    qkv_out,
-    out_taken,
-    out_sums,
-    out_moved,
-    qkv_taken,
-    qkv_sums,
-    qkv_moved,
-    grad_resid,
-    query_weight,
-    heads_out,
-    grad_gain,
-    gain_parts,
-    gain_dp,
-    gain_sum,
-    gain_z,
-    grad_qkv,
-    out_stage,
-    qkv_stage,
-    pair_out,
-    pair_qkv,
-    bias,
-    dy,
-    do_t,
-    do_h,
-    dq_t,
-    dk,
-    dv,
-    part,
-    held,
-    total,
-    own,
-    near,
-    in_sem,
-    tok_sem,
-    red_send,
-    red_recv,
-    gat_send,
-    gat_recv,
-    gat_stay,
-    pair_sem,
-    late_sem,
-    gain_send,
-    gain_recv,
-    zsum_send,
-    zsum_recv,
-    *dp_sems,
-):
-    length, width = tokens.shape
-    chunk = length // chunks
-    wide = length // big
-    sub = chunks // big
-    piece = chunk // 4
-    heads = query_t.shape[0] // HD
-    factor = HD ** (-0.5)
-    line = Line(piece)
-    red = Reduce(line, part, held, total, red_send, red_recv)
-    gat = Gather(line, own, tokens_grad, gat_send, gat_recv, gat_stay)
-    order = list(reversed(range(big)))
-
-    def load(c, slot):
-        return pltpu.make_async_copy(
-            branch.at[c * wide : (c + 1) * wide], dy.at[slot], in_sem.at[slot]
-        )
-
-    def near_copy(c):
-        return pltpu.make_async_copy(tokens.at[gat.mine(c)], near.at[c], tok_sem.at[c])
-
-    load(order[0], 0).start()
-    for c in range(chunks):
-        near_copy(c).start()
-    late = [
-        pltpu.make_async_copy(src, dst, late_sem.at[i])
-        for i, (src, dst) in enumerate(
-            ((query_in, query_weight), (resid_in, grad_resid), (heads_in, heads_out))
-        )
-    ]
-    for copy in late:
-        copy.start()
-    line.greet(dps, every=True)
-    grad_gain[...] = jnp.zeros_like(grad_gain)
-    dk[...] = jnp.zeros_like(dk)
-    dv[...] = jnp.zeros_like(dv)
-
-    def enter(i):
-        c, slot = order[i], i % 2
-        load(c, slot).wait()
-        if i + 1 < big:
-            load(order[i + 1], 1 - slot).start()
+            for k in range(chunks):
+                gat_a.complete(k)
+        branch_load(c, slot).start()
+        for k in range(c * sub, (c + 1) * sub):
+            red_a.close(k)
+            gat_a.close(k)
+        if i == 0:
+            for copy in late:
+                copy.wait()
+        branch_load(c, slot).wait()
         keys_n = (c + 1) * wide
         bias[:keys_n, :] = visible_bias(seg_row[...], seg_key[...], c, wide)
-        grad_heads = nt(dy[slot], out_weight[...])
-        do_t[...] = grad_heads.T.astype(BF)
-        for h in range(heads):
-            do_h[h] = grad_heads[:, h * HD : (h + 1) * HD].astype(BF)
-
-    def attend(i, begin, end):
+        for k in range(2):
+            grad_heads = nt(hid[slot], dy[k])
+            do_t[k * half_lanes : (k + 1) * half_lanes, :] = grad_heads.T.astype(BF)
+
+    def back_attend(i, begin, end):
         c = order[i]
         keys_n = (c + 1) * wide
         cols = slice(c * wide, keys_n)
@@ -984,67 +927,66 @@
             grad_probs = nn(values[:keys_n, :], do_t[here, :])
             delta = jnp.sum(probs * grad_probs, axis=0, keepdims=True)
             grad_scores = (probs * (grad_probs - delta)).astype(BF)
-            dv[:keys_n, :] += nn(probs.astype(BF), do_h[h])
+            dv[:keys_n, :] += nn(probs.astype(BF), do_t[here, :].T)
             dk[:keys_n, :] += nn(grad_scores, query_t[here, cols].T)
             grad = nn(keys_t[:, :keys_n], grad_scores) * factor
-            dq_t[here, :] = unrope(grad, cosine[:, cols], sine[:, cols])
+            heads_t[here, :] = unrope(grad, cosine[:, cols], sine[:, cols])
             return carry
 
         lax.fori_loop(begin, end, head, 0)
 
-    def leave(i):
+    def back_leave(i):
         c = order[i]
         cols = slice(c * wide, (c + 1) * wide)
-        lanes = heads * HD
-        grad_qkv[cols, :lanes] = dq_t[...].T.astype(BF)
+        wg[cols, :lanes] = heads_t[...].T.astype(BF)
         grad_k = unrope(dk[cols, :].T, cosine[:, cols], sine[:, cols]).T
-        grad_qkv[cols, lanes:] = jnp.concatenate([grad_k, dv[cols, :]], axis=1).astype(BF)
-        if i == 0:
-            for copy in late:
-                copy.wait()
-        step = min(512, width)
+        wg[cols, lanes : lanes + kv] = jnp.concatenate([grad_k, dv[cols, :]], axis=1).astype(BF)
+        step = 512
         for n in range(0, width, step):
             here = slice(n, n + step)
-            value = nt(grad_qkv[cols, :lanes], query_weight[here, :])
-            put(part, c, here, value + nt(grad_qkv[cols, lanes:], kv_weight[here, :]))
-
-    def tasks(i):
-        half = heads // 2
+            k, row = n // length, length + n % length
+            rows = slice(row, row + step)
+            value = nt(wg[cols, :lanes], wu[rows, k * lanes : (k + 1) * lanes])
+            at = 2 * lanes + k * kv
+            value = value + nt(wg[cols, lanes : lanes + kv], wu[rows, at : at + kv])
+            put(part_a, c, here, value)
+
+    def back_tasks(i):
+        quarter = heads // 4
         return [
-            functools.partial(enter, i),
-            functools.partial(attend, i, 0, half),
-            functools.partial(attend, i, half, heads),
-            functools.partial(leave, i),
+            functools.partial(back_enter, i),
+            *[functools.partial(back_attend, i, k * quarter, (k + 1) * quarter) for k in range(4)],
+            functools.partial(back_leave, i),
         ]
 
-    spread_out = Spread(line, out_stage, out_out, out_taken, out_sums, out_moved, dp_sems[:5])
-    spread_qkv = Spread(line, qkv_stage, qkv_out, qkv_taken, qkv_sums, qkv_moved, dp_sems[5:])
-    pair = 2 * width // dps
-    groups = dps // 2
-    units_order = list(range(1, groups)) + [0]
-
-    def pair_load(j, slot, src, dst, number):
-        cols = pl.ds(pl.multiple_of(line.group(j) * pair, pair), pair)
-        return pltpu.make_async_copy(src.at[:, cols], dst.at[slot], pair_sem.at[slot, number])
+    def one_load(n, src, at):
+        slot = n % 2
+        cols = pl.ds(pl.multiple_of(line.group(units_order[n]) * pair, pair), pair)
+        at = 2 * slot * pair + at * pair
+        return pltpu.make_async_copy(
+            src.at[:, cols], wd.at[:length, at : at + pair], pair_sem.at[slot, 0]
+        )
 
     def unit_out(n):
-        j, slot = units_order[n], n % 2
-        pair_load(j, slot, branch, pair_out, 0).wait()
+        at = 2 * (n % 2) * pair + pair
+        if n == 0:
+            one_load(n, branch, 1).start()
+        one_load(n, branch, 1).wait()
         if n + 1 < groups:
-            pair_load(units_order[n + 1], 1 - slot, branch, pair_out, 0).start()
-        halves(out_stage, tn(heads_out[...], pair_out[slot]), 1)
-        spread_out.give(j).start()
+            one_load(n + 1, branch, 1).start()
+        halves(out_stage, tn(heads_out[...], wd[:length, at : at + pair]), 1)
+        spread_out.give(units_order[n]).start()
 
     def unit_qkv(n):
-        j, slot = units_order[n], n % 2
-        pair_load(j, slot, hidden1, pair_qkv, 1).wait()
+        at = 2 * (n % 2) * pair
+        if n == 0:
+            one_load(n, hidden1, 0).start()
+        one_load(n, hidden1, 0).wait()
         if n + 1 < groups:
-            pair_load(units_order[n + 1], 1 - slot, hidden1, pair_qkv, 1).start()
-        halves(qkv_stage, tn(pair_qkv[slot], grad_qkv[...]), 0)
-        spread_qkv.give(j).start()
-
-    pair_load(units_order[0], 0, branch, pair_out, 0).start()
-    pair_load(units_order[0], 0, hidden1, pair_qkv, 1).start()
+            one_load(n + 1, hidden1, 0).start()
+        halves(qkv_stage, tn(wd[:length, at : at + pair], wg[:length, : lanes + kv]), 0)
+        spread_qkv.give(units_order[n]).start()
+
     work_out, work_qkv = [], []
     for n in range(groups):
         work_out.append(functools.partial(unit_out, n))
@@ -1052,20 +994,31 @@
         work_qkv.append(functools.partial(unit_qkv, n))
         work_qkv += merged([spread_qkv], units_order[n])
 
-    def done(c):
-        near_copy(c).wait()
+    exits = [
+        pltpu.make_async_copy(src, dst, exit_sem.at[i])
+        for i, (src, dst) in enumerate(
+            (
+                (rows_acc, gate_out),
+                (rows_acc, up_out),
+                (cols_acc, down_out),
+                (out_acc, out_out),
+                (qkv_acc.at[:, :lanes], query_out),
+            )
+        )
+    ]
+
+    def done_q(c):
+        near_copy(c, tokens).wait()
         grad = total[...]
         vector = near[c].astype(F32)
         scale = normed(vector)
-        scaled = grad * gain[...]
+        scaled = grad * gain1[...]
         inner = jnp.mean(scaled * vector, axis=-1, keepdims=True)
-        grad_gain[...] += jnp.sum(grad * vector * scale, axis=0, keepdims=True)
+        grad_gain1[...] += jnp.sum(grad * vector * scale, axis=0, keepdims=True)
         back = grad_resid[c] + scale * scaled - vector * (scale * scale * scale) * inner
-        own[c] = back.astype(BF)
+        own_a[c] = back.astype(BF)
 
     block = width // dps
-    slots = [(red, gat, done, c) for c in reversed(range(chunks))]
-
     def gain_move(j):
         return pltpu.make_async_remote_copy(
             src_ref=gain_parts.at[line.dp_peer(j)],
@@ -1087,7 +1040,7 @@
         )
 
     def gains_dp():
-        both = jnp.concatenate([grad_gain[...], other_gain[...]], axis=0)
+        both = jnp.concatenate([grad_gain1[...], grad_gain2[...]], axis=0)
         for d in range(dps):
             gain_parts[d] = both[:, d * block : (d + 1) * block]
         for j in range(1, dps):
@@ -1110,31 +1063,53 @@
             value = value + gain_z[j]
         gains_out[...] = value
 
+    slots = [(red_p, gat_p, norm, c) for c in range(chunks)]
+    slots += [(red_a, gat_a, done_a, c) for c in range(chunks)]
+    slots += [(red_b, gat_b, done_b, c) for c in range(chunks)]
+    slots += [(red_q, gat_q, done_q, c) for c in reversed(range(chunks))]
+    count = len(slots)
     plan = {}
-    for i in range(1, big):
-        schedule(plan, tasks(i), sub * (i - 1), 4 // sub)
-    schedule(plan, work_out, 1, 3)
-    schedule(plan, work_qkv, sub * (big - 1), 4)
+    for n in range(1, big):
+        schedule(plan, attn_tasks(n), sub * (n - 1), 4 // sub)
+    for n in range(big):
+        schedule(plan, feed_tasks(n), sub * (big - 1 + n), 6 // sub)
+    first = sub * (2 * big - 1)
+    schedule(plan, [turn], first, 1)
+    schedule(plan, after, first + 1, -(-len(after) // 5))
+    first = 2 * chunks + 3
+    for i in range(big):
+        schedule(plan, back_tasks(i), first + sub * i, 6 // sub)
+    schedule(plan, work_out, first + 2, -(-len(work_out) // 8))
+    ends = [
+        finished(spreads[0], exits[:1]),
+        finished(spreads[2], exits[2:3]),
+        finished(spreads[1], exits[1:2], exits[:1]),
+    ]
+    schedule(plan, ends, 3 * chunks + 3, 1)
+    first += sub * big
+    schedule(plan, work_qkv, first, -(-len(work_qkv) // 4))
+    schedule(plan, [finished(spread_out, exits[3:4])], count + 1, 1)
 
     def begin(i):
         if i == 0:
-            for task in tasks(0):
+            for task in attn_tasks(0):
                 task()
-        if i < chunks:
-            red.start(slots[i][3])
-        if i == chunks + 2:
+        if i < count:
+            red, _, _, c = slots[i]
+            red.start(c)
+        if i == count + 2:
             gains_dp()
-        if i == chunks + 3:
+        if i == count + 3:
             gains_line()
 
     drive(slots, begin, plan)
-    for i in sorted(plan):
-        if i >= chunks + 4:
-            for task in plan[i]:
-                task()
+    finished(spread_qkv, exits[4:])()
+    key_out[...] = qkv_acc[:, lanes : lanes + HD]
+    value_out[...] = qkv_acc[:, lanes + HD :]
     gains_end()
-    finished([spread_out, spread_qkv])
-    for red, gat, done, c in slots:
+    for copy in exits[1:]:
+        copy.wait()
+    for red, gat, done, c in slots[2 * chunks :]:
         red.close(c)
         gat.complete(c)
         gat.close(c)
@@ -1167,7 +1142,7 @@
 
 def spread_shapes(groups, rows, cols):
     dma = pltpu.SemaphoreType.DMA
-    outs = [(VMEM, (rows, cols), F32)]
+    outs = [(ANY, (rows, cols), F32)]
     boxes = [(ANY, (groups, rows, cols), BF)] * 3
     stage = pltpu.VMEM((2, rows, cols), BF)
     return outs, boxes, stage, [dma((groups,))] * 4 + [dma((2,))]
@@ -1224,25 +1199,11 @@
     near = pltpu.VMEM((chunks, piece, width), BF)
     by_rows = spread_shapes(groups, block, units)
     by_cols = spread_shapes(groups, units, block)
+    for_out = spread_shapes(groups, lanes, block)
+    for_qkv = spread_shapes(groups, block, lanes + 2 * HD)
     kv_weight = jnp.concatenate([key_weight, value_weight], axis=1)
-    (
-        mixed,
-        branch,
-        hidden1,
-        grad_resid,
-        grad_gain2,
-        heads_out,
-        logs,
-        query_t,
-        keys,
-        keys_t,
-        values,
-        gate_grad,
-        up_grad,
-        down_grad,
-        *_,
-    ) = call(
-        functools.partial(front_kernel, chunks, big, dps),
+    outs = call(
+        functools.partial(layer_kernel, chunks, big, dps),
         [
             (ANY, tokens),
             (ANY, cotangent),
@@ -1263,23 +1224,21 @@
         [
             (ANY, (length, width), BF),
             (ANY, (length, width), BF),
-            (ANY, (length, width), BF),
-            (VMEM, (chunks, piece, width), F32),
-            (VMEM, (1, width), F32),
-            (VMEM, (length, lanes), BF),
-            (VMEM, (heads, 1, length), F32),
-            (VMEM, (lanes, length), BF),
-            (VMEM, (length, HD), BF),
-            (VMEM, (HD, length), BF),
-            (VMEM, (length, HD), BF),
+            (VMEM, (2, block), F32),
+            (ANY, (block, lanes), F32),
+            (VMEM, (block, HD), F32),
+            (VMEM, (block, HD), F32),
+            *for_out[0],
             *by_rows[0],
             *by_rows[0],
             *by_cols[0],
-            (ANY, (length, width), BF),
+            *[(ANY, (length, width), BF)] * 3,
             *[(ANY, (length, units), BF)] * 3,
             *by_rows[1],
             *by_rows[1],
             *by_cols[1],
+            *for_out[1],
+            *for_qkv[1],
         ],
         [
             pltpu.VMEM((width, units), BF),
@@ -1292,6 +1251,28 @@
             pltpu.VMEM((2, wide, units), BF),
             *[pltpu.VMEM((2, 16, units), BF) if block == wide else by_rows[2]] * 2,
             by_cols[2],
+            for_out[2],
+            for_qkv[2],
+            pltpu.VMEM((block, units), F32),
+            pltpu.VMEM((units, block), F32),
+            pltpu.VMEM((lanes, block), F32),
+            pltpu.VMEM((block, lanes + 2 * HD), F32),
+            pltpu.VMEM((length, lanes), BF),
+            pltpu.VMEM((heads, 1, length), F32),
+            pltpu.VMEM((lanes, length), BF),
+            pltpu.VMEM((length, HD), BF),
+            pltpu.VMEM((HD, length), BF),
+            pltpu.VMEM((length, HD), BF),
+            pltpu.VMEM((lanes, wide), BF),
+            pltpu.VMEM((length, HD), F32),
+            pltpu.VMEM((length, HD), F32),
+            pltpu.VMEM((chunks, piece, width), F32),
+            pltpu.VMEM((1, width), F32),
+            pltpu.VMEM((1, width), F32),
+            pltpu.VMEM((dps, 2, block), F32),
+            pltpu.VMEM((dps, 2, block), F32),
+            pltpu.VMEM((2, block), F32),
+            pltpu.VMEM((4, 2, block), F32),
             pltpu.VMEM((HD, length), BF),
             pltpu.VMEM((length, wide), F32),
             pltpu.VMEM((lanes, wide), F32),
@@ -1310,105 +1291,27 @@
             dma((chunks,)),
             dma((3,)),
             dma((2, 2)),
+            dma((6,)),
+            dma((5,)),
+            dma((dps,)),
+            dma((dps,)),
+            dma((4,)),
+            dma((4,)),
+            *sems,
             *sems,
             *sems,
             *sems,
             *by_rows[3],
             *by_rows[3],
             *by_cols[3],
+            *for_out[3],
+            *for_qkv[3],
         ],
         0,
-        5 * 10**10,
+        8 * 10**10,
     )
-
-    by_cols = spread_shapes(groups, lanes, block)
-    by_rows = spread_shapes(groups, block, lanes + 2 * HD)
-    tokens_grad, gains, out_grad, qkv_grad, *_ = call(
-        functools.partial(back_kernel, chunks, big, dps),
-        [
-            (ANY, branch),
-            (ANY, tokens),
-            (ANY, grad_resid),
-            (VMEM, gain1),
-            (VMEM, seg_row),
-            (VMEM, seg_key),
-            (VMEM, cosine),
-            (VMEM, sine),
-            (VMEM, query_t),
-            (VMEM, keys),
-            (VMEM, keys_t),
-            (VMEM, values),
-            (VMEM, logs),
-            (VMEM, out_weight),
-            (ANY, query_weight),
-            (VMEM, kv_weight),
-            (VMEM, grad_gain2),
-            (ANY, heads_out),
-            (ANY, hidden1),
-        ],
-        [
-            (ANY, (length, width), BF),
-            (VMEM, (2, block), F32),
-            *by_cols[0],
-            *by_rows[0],
-            *by_cols[1],
-            *by_rows[1],
-        ],
-        [
-            pltpu.VMEM((chunks, piece, width), F32),
-            pltpu.VMEM((width, lanes), BF),
-            pltpu.VMEM((length, lanes), BF),
-            pltpu.VMEM((1, width), F32),
-            pltpu.VMEM((dps, 2, block), F32),
-            pltpu.VMEM((dps, 2, block), F32),
-            pltpu.VMEM((2, block), F32),
-            pltpu.VMEM((4, 2, block), F32),
-            pltpu.VMEM((length, lanes + 2 * HD), BF),
-            by_cols[2],
-            by_rows[2],
-            pltpu.VMEM((2, length, 2 * block), BF),
-            pltpu.VMEM((2, length, 2 * block), BF),
-            pltpu.VMEM((length, wide), F32),
-            pltpu.VMEM((2, wide, width), BF),
-            pltpu.VMEM((lanes, wide), BF),
-            pltpu.VMEM((heads, wide, HD), BF),
-            pltpu.VMEM((lanes, wide), F32),
-            pltpu.VMEM((length, HD), F32),
-            pltpu.VMEM((length, HD), F32),
-            buffers[0],
-            buffers[1],
-            total,
-            buffers[2],
-            near,
-            dma((2,)),
-            dma((chunks,)),
-            *sems,
-            dma((2, 2)),
-            dma((3,)),
-            dma((dps,)),
-            dma((dps,)),
-            dma((4,)),
-            dma((4,)),
-            *by_cols[3],
-            *by_rows[3],
-        ],
-        1,
-        2 * 10**10,
-    )
-
-    return (
-        mixed,
-        tokens_grad,
-        gains[0],
-        gains[1],
-        qkv_grad[:, :lanes],
-        qkv_grad[:, lanes : lanes + HD],
-        qkv_grad[:, lanes + HD :],
-        out_grad,
-        gate_grad,
-        up_grad,
-        down_grad,
-    )
+    mixed, tokens_grad, gains = outs[:3]
+    return (mixed, tokens_grad, gains[0], gains[1], *outs[3:10])
 
 
 def solution(mesh):

time: 490 us -> 442 us (0.902)
  Pallas kernels: 453 us -> 406 us
    pallas_call x2 -> x1, Pallas kernels: 453 us -> 406 us  [call(): pl.pallas_call(kernel, in_specs=[spec for spec, _ in ins], out_specs=[spe...]
    unnamed x20 -> x23, local copies, waits for them, and re-layouts: 15.1 us -> 17.7 us
where the time goes in v4:
time: 442 us; the launch traced here: 433 us
  Pallas kernels  406 us (92%)
  local copies, waits for them, and re-layouts  20 us (5%)
  other arithmetic  5.19 us (1%)
    pallas_call x1, Pallas kernels, call(): pl.pallas_call(kernel, in_specs=[spec for spec, _ in ins], out_specs=[spe...  406 us
    unnamed x23, local copies, waits for them, and re-layouts  17.7 us

profile of v4, /device:TPU:0, one launch (start us, length us, event | category | flops | bytes accessed | tf_op | source)
XLA Modules:
  0.0 433.3 jit_solution(1050333383451293724)
XLA Ops:
  1.3 0.7 fusion.1
  2.0 1.3 convert_reduce_fusion
  3.3 1.2 multiply_sine_fusion
  4.6 1.0 copy.35.seg_key
  5.6 1.2 copy.33
  6.8 1.2 copy.34
  8.1 1.1 pad_maximum_fusion.kv_weight
  9.1 0.8 fusion.live
  10.0 406.3 %shard_map.212 = (bf16[1024,2048]{1,0:T(8,128)(2,1)}, bf16[1024,2048]{1,0:T(8,128)(2,1)}, f32[2,256]{1,0:T(2,128)}, f32[256,512]{1,0:T(8,128)}, f32[256,64]{1,0:...) custom-call(bf16[1024,2048]{1,0:T(8,128)(2,1)} %tokens.1, ...), custom_call_target="tpu_custom_call" | custom-call | flops 80000000000 | bytes 80000000 | tf_op jit(solution)/shard_map/pallas_call | solution.py:1119
  416.3 1.3 fusion.2
  417.6 1.6 copy.36
  419.3 1.6 copy.37
  420.9 0.0 copy-start
  420.9 4.9 %copy.46 = bf16[1024,2048]{1,0:T(8,128)(2,1)} copy(bf16[1024,2048]{1,0:T(8,128)(2,1)} %get-tuple-element.79) | data formatting | bytes 8388608
  425.8 0.0 copy-done
  425.8 0.0 copy-start.5
  425.8 0.0 copy-start.4
  425.8 0.0 copy-start.3
  425.8 2.1 copy.47
  428.0 0.0 copy-done.5
  428.0 0.0 copy-start.2
  428.0 0.8 copy.48
  428.8 0.0 copy-done.4
  428.8 0.8 copy.49
  429.6 0.0 copy-done.3
  429.6 0.0 copy-start.1
  429.6 1.1 copy.50
  430.7 0.0 copy-done.2
  430.7 1.1 copy.51
  431.8 0.0 copy-done.1
  431.8 1.1 copy.52
  (2 shorter events, 0.0 us)
Async XLA Ops:
  420.9 4.9 %copy-start = (bf16[1024,2048]{1,0:T(8,128)(2,1)S(1)}, bf16[1024,2048]{1,0:T(8,128)(2,1)}, u32[]{:S(2)}) copy-start(bf16[1024,2048]{1,0:T(8,128)(2,1)} %get-tuple-element.80) | copy-start | bytes 12582916
  425.8 2.1 copy-start.5
  425.8 2.9 copy-start.4
  425.8 3.7 copy-start.3
  428.0 2.7 copy-start.2
  429.6 2.2 copy-start.1
